TPU v7x, 512 devices: a whole 4x8x8 slice. The times are simulated.
512 devices in a mesh: group: 64 (over y_hi, x, z), loop: 8 (over y_lo, core).
Axes of the slice: x: 4, y: 8 (y_hi: 2, y_lo: 4; y = y_hi * 4 + y_lo), z: 8, core: 2. Of those that a mesh axis runs over, the one named last changes fastest.
Arguments:
- queries: float32 [131072, 1024], P(('loop', 'group')), may hold values from -2 to 2
- keys: float32 [131072, 1024], P(('loop', 'group')), may hold values from -1 to 1
- pattern: int32 [512, 5], P(('loop', 'group')), may hold values from 0 to 1, as said below
- positive: int32 [131072], P(('loop', 'group')), may hold values from 0 to 1279, as said below
Outputs:
- loss: float32 [131072], P(('loop', 'group'))
- grad_queries: float32 [131072, 1024], P(('loop', 'group'))
- grad_keys: float32 [131072, 1024], P(('loop', 'group'))
Inputs may be any that keep to these rules, and one draw needn't show every extreme that they name: `pattern`: 0 or 1; column 0 is always 1; column 3 is 0 for tiles of band 0 and column 4 is 0 for tiles of band 64 - 1. The neighbour column positive // 256 of the query's tile is allowed by pattern.
All inputs are finite; a program needn't handle non-finite values.
Results may differ from a plain program's by a relative error of at most 0.00045.
Values sent between devices are 32-bit elements; how exact they have to be, the bound alone decides.
No kernel may reach another device: no remote copies, remote signals or barrier semaphores. Data moves between devices by JAX's collectives and lax.ppermute only.
A program may use at most 64 MiB of HBM per device.

v0:
```python
import math

import jax
import jax.numpy as jnp
from jax import lax
from jax.sharding import PartitionSpec as P

HIGH = lax.Precision.HIGHEST


def with_halo(cells, sides, width, closed):
    for axis, dim in sides:
        count = lax.axis_size(axis)
        ends = count if closed else count - 1
        head = lax.slice_in_dim(cells, 0, width, axis=dim)
        tail = lax.slice_in_dim(cells, cells.shape[dim] - width, cells.shape[dim], axis=dim)
        cells = jnp.concatenate(
            [
                lax.ppermute(tail, axis, [(i, (i + 1) % count) for i in range(ends)]),
                cells,
                lax.ppermute(head, axis, [((i + 1) % count, i) for i in range(ends)]),
            ],
            axis=dim,
        )
    return cells


def local(queries, keys, pattern, positive):
    tile_rows, features = queries.shape
    neighbours = pattern.shape[1]
    sharpness = math.sqrt(features)
    allowed = pattern[0] > 0
    sector_keys = with_halo(keys[None], (("loop", 0),), 1, True)
    band_keys = with_halo(keys[None], (("group", 0),), 1, False)
    stacked = jnp.stack([keys, sector_keys[0], sector_keys[2], band_keys[0], band_keys[2]])
    scores = jnp.einsum("id,ojd->ioj", queries, stacked, precision=HIGH) * sharpness
    mask = allowed[None, :, None]
    masked = jnp.where(mask, scores, -jnp.inf)
    highest = jnp.max(masked, axis=(1, 2))
    partition = jnp.sum(jnp.where(mask, jnp.exp(masked - highest[:, None, None]), 0.0), axis=(1, 2))
    log_total = highest + jnp.log(partition)
    slot_ids = jnp.arange(neighbours * tile_rows, dtype=jnp.int32)
    is_positive = (slot_ids[None, :] == positive[:, None]).reshape(tile_rows, neighbours, tile_rows)
    positive_score = jnp.sum(jnp.where(is_positive, scores, 0.0), axis=(1, 2))
    loss = log_total - positive_score
    probs = jnp.where(mask, jnp.exp(masked - log_total[:, None, None]), 0.0)
    weights = probs - is_positive.astype(jnp.float32)
    grad_queries = jnp.einsum("ioj,ojd->id", weights, stacked, precision=HIGH) * sharpness
    terms = jnp.einsum("ioj,id->ojd", weights, queries, precision=HIGH) * sharpness
    sector_back = with_halo(jnp.stack([terms[1], terms[2]]), (("loop", 0),), 1, True)
    band_back = with_halo(jnp.stack([terms[3], terms[4]]), (("group", 0),), 1, False)
    grad_keys = terms[0] + sector_back[0] + sector_back[3] + band_back[0] + band_back[3]
    return (loss, grad_queries, grad_keys)


def solution(mesh):
    placed = (
        P(("loop", "group"), None),
        P(("loop", "group"), None),
        P(("loop", "group"), None),
        P(("loop", "group")),
    )
    return jax.shard_map(
        local,
        mesh=mesh,
        in_specs=placed,
        out_specs=(P(("loop", "group")), P(("loop", "group"), None), P(("loop", "group"), None)),
        check_vma=False,
    )
```

profile of v0, /device:TPU:455, one launch (start us, length us, event | category | flops | bytes accessed | tf_op | source)
XLA Modules:
  0.0 152.5 jit_solution(13523184878752259490)
XLA Ops:
  0.6 0.0 copy-start
  0.6 3.9 %collective-permute-start = (f32[1,256,1024]{2,1,0:T(8,128)}, f32[1,256,1024]{2,1,0:T(8,128)S(1)}, u32[]{:S(2)}, u32[]{:S(2)}) collective-permute-start(f32[1,256,1024]{2,1,0:T(8,128)} %bitcast.21), channel_id=1, source_target_pairs={{0,1},{1,2},{2,3},{3,4},{4,5},{5,6},{6,7},{7,0},{8,9},{9,10},{10,1... | collective-permute-start | bytes 3145736 | tf_op jit(solution)/shard_map/ppermute | solution.py:19
  4.6 1.9 %collective-permute-start.1 = (f32[1,256,1024]{2,1,0:T(8,128)}, f32[1,256,1024]{2,1,0:T(8,128)S(1)}, u32[]{:S(2)}, u32[]{:S(2)}) collective-permute-start(f32[1,256,1024]{2,1,0:T(8,128)} %bitcast.22), channel_id=1, source_target_pairs={{1,0},{2,1},{3,2},{4,3},{5,4},{6,5},{7,6},{0,7},{9,8},{10,9},{11,1... | collective-permute-start | bytes 3145736 | tf_op jit(solution)/shard_map/ppermute | solution.py:21
  6.5 1.9 %collective-permute-start.2 = (f32[1,256,1024]{2,1,0:T(8,128)}, f32[1,256,1024]{2,1,0:T(8,128)S(1)}, u32[]{:S(2)}, u32[]{:S(2)}) collective-permute-start(f32[1,256,1024]{2,1,0:T(8,128)} %bitcast.23), channel_id=1, source_target_pairs={{0,8},{8,16},{16,24},{24,32},{32,40},{40,48},{48,56},{56,64},{64,7... | collective-permute-start | bytes 3145736 | tf_op jit(solution)/shard_map/ppermute | solution.py:19
  8.4 3.4 %collective-permute-start.3 = (f32[1,256,1024]{2,1,0:T(8,128)}, f32[1,256,1024]{2,1,0:T(8,128)S(1)}, u32[]{:S(2)}, u32[]{:S(2)}) collective-permute-start(f32[1,256,1024]{2,1,0:T(8,128)} %bitcast.24), channel_id=1, source_target_pairs={{8,0},{16,8},{24,16},{32,24},{40,32},{48,40},{56,48},{64,56},{72,6... | collective-permute-start | bytes 3145736 | tf_op jit(solution)/shard_map/ppermute | solution.py:21
  11.8 0.7 compare_bitcast_fusion
  12.5 1.3 constant_dynamic-update-slice_fusion.4
  13.8 9.5 %collective-permute-done = f32[1,256,1024]{2,1,0:T(8,128)S(1)} collective-permute-done((f32[1,256,1024]{2,1,0:T(8,128)}, f32[1,256,1024]{2,1,0:T(8,128)S(1)}, u32[]{:S(2)}, u32[]{:S(2)}) %collective-permute-start) | collective-permute-done | bytes 1048608 | tf_op jit(solution)/shard_map/ppermute | solution.py:19
  23.3 0.1 constant_dynamic-update-slice_fusion.3
  23.4 40.4 %collective-permute-done.1 = f32[1,256,1024]{2,1,0:T(8,128)S(1)} collective-permute-done((f32[1,256,1024]{2,1,0:T(8,128)}, f32[1,256,1024]{2,1,0:T(8,128)S(1)}, u32[]{:S(2)}, u32[]{:S(2)}) %collective-permute-start.1) | collective-permute-done | bytes 1048608 | tf_op jit(solution)/shard_map/ppermute | solution.py:21
  63.7 0.1 constant_dynamic-update-slice_fusion.2
  63.8 0.0 collective-permute-done.2
  63.8 0.1 constant_dynamic-update-slice_fusion.1
  63.9 0.0 collective-permute-done.3
  63.9 0.1 constant_dynamic-update-slice_fusion
  64.0 0.0 copy-start.1
  64.0 4.3 %select_reduce_fusion.1 = (f32[256]{0:T(256)S(1)}, f32[256,5,256]{0,2,1:T(8,128)S(1)}) fusion(pred[5]{0:T(512)(128)(4,1)S(1)} %compare_bitcast_fusion, f32[5,256,1024]{2,1,0:T(8,128)S(1)} %constant_dynamic-update-slice_fusion, f32[256,1024]{1,0:T(8,128)S(1)} %copy-done), kind=kOutput, calls=%fused_computation.10 | convolution fusion | flops 4027514624 | bytes 7603205 | tf_op jit(solution)/shard_map/id,ojd->ioj/dot_general | solution.py:36
  68.4 0.0 copy-done.1
  68.4 0.5 fusion.2
  68.8 0.6 fusion.28
  69.4 4.6 %broadcast_multiply_fusion = f32[5,256,1024]{2,1,0:T(8,128)S(1)} fusion(f32[256,1024]{1,0:T(8,128)S(1)} %copy-done, f32[256,5,256]{0,2,1:T(8,128)S(1)} %get-tuple-element.12, f32[256]{0:T(256)S(1)} %get-tuple-element.6, s32[256]{0:T(256)S(1)} %copy-done.1, s32[5,256]{1,0:T(8,128)S(1)} %multiply_add_fusion, pred[5]{0:T(512)(128)(4,1)S(1)} %compare_bitcast_fusion), kind=kOutput, calls=%fused_computation | convolution fusion | flops 4029808640 | bytes 7609349 | tf_op jit(solution)/shard_map/ioj,id->ojd/dot_general | solution.py:49
  74.0 0.6 fusion.29
  74.6 1.9 %collective-permute-start.7 = (f32[1,256,1024]{2,1,0:T(8,128)S(1)}, f32[1,256,1024]{2,1,0:T(8,128)S(1)}, u32[]{:S(2)}, u32[]{:S(2)}) collective-permute-start(f32[1,256,1024]{2,1,0:T(8,128)S(1)} %get-tuple-element.8), channel_id=1, source_target_pairs={{8,0},{16,8},{24,16},{32,24},{40,32},{48,40},{56,48},{64,56},{72,6... | collective-permute-start | bytes 3145736 | tf_op jit(solution)/shard_map/ppermute | solution.py:21
  76.5 11.5 %collective-permute-start.6 = (f32[1,256,1024]{2,1,0:T(8,128)S(1)}, f32[1,256,1024]{2,1,0:T(8,128)S(1)}, u32[]{:S(2)}, u32[]{:S(2)}) collective-permute-start(f32[1,256,1024]{2,1,0:T(8,128)S(1)} %get-tuple-element.9), channel_id=1, source_target_pairs={{0,8},{8,16},{16,24},{24,32},{32,40},{40,48},{48,56},{56,64},{64,7... | collective-permute-start | bytes 3145736 | tf_op jit(solution)/shard_map/ppermute | solution.py:19
  88.0 1.9 %collective-permute-start.5 = (f32[1,256,1024]{2,1,0:T(8,128)S(1)}, f32[1,256,1024]{2,1,0:T(8,128)S(1)}, u32[]{:S(2)}, u32[]{:S(2)}) collective-permute-start(f32[1,256,1024]{2,1,0:T(8,128)S(1)} %get-tuple-element.10), channel_id=1, source_target_pairs={{1,0},{2,1},{3,2},{4,3},{5,4},{6,5},{7,6},{0,7},{9,8},{10,9},{11,1... | collective-permute-start | bytes 3145736 | tf_op jit(solution)/shard_map/ppermute | solution.py:21
  89.9 41.3 %collective-permute-start.4 = (f32[1,256,1024]{2,1,0:T(8,128)S(1)}, f32[1,256,1024]{2,1,0:T(8,128)S(1)}, u32[]{:S(2)}, u32[]{:S(2)}) collective-permute-start(f32[1,256,1024]{2,1,0:T(8,128)S(1)} %get-tuple-element.7), channel_id=1, source_target_pairs={{0,1},{1,2},{2,3},{3,4},{4,5},{5,6},{6,7},{7,0},{8,9},{9,10},{10,1... | collective-permute-start | bytes 3145736 | tf_op jit(solution)/shard_map/ppermute | solution.py:19
  131.3 5.8 %fusion.1 = f32[256,1024]{1,0:T(8,128)} fusion(f32[5,256,1024]{2,1,0:T(8,128)S(1)} %constant_dynamic-update-slice_fusion, f32[256,5,256]{0,2,1:T(8,128)S(1)} %get-tuple-element.12, f32[256]{0:T(256)S(1)} %get-tuple-element.6, s32[256]{0:T(256)S(1)} %copy-done.1, s32[5,256]{1,0:T(8,128)S(1)} %multiply_add_fusion, pred[5]{0:T(512)(128)(4,1)S(1)} %compare_bitcast_fusion), kind=kOutput, calls=%fused_computation.6 | convolution fusion | flops 4028760064 | bytes 7609349 | tf_op jit(solution)/shard_map/ioj,ojd->id/dot_general | solution.py:48
  137.1 0.0 collective-permute-done.7
  137.1 0.0 collective-permute-done.6
  137.1 13.8 %collective-permute-done.5 = f32[1,256,1024]{2,1,0:T(8,128)S(1)} collective-permute-done((f32[1,256,1024]{2,1,0:T(8,128)S(1)}, f32[1,256,1024]{2,1,0:T(8,128)S(1)}, u32[]{:S(2)}, u32[]{:S(2)}) %collective-permute-start.5) | collective-permute-done | bytes 1048608 | tf_op jit(solution)/shard_map/ppermute | solution.py:21
  150.9 0.0 collective-permute-done.4
  151.0 1.5 %fusion.7 = f32[256,1024]{1,0:T(8,128)} fusion(f32[1,256,1024]{2,1,0:T(8,128)S(1)} %collective-permute-done.7, f32[1,256,1024]{2,1,0:T(8,128)S(1)} %collective-permute-done.6, f32[1,256,1024]{2,1,0:T(8,128)S(1)} %collective-permute-done.5, f32[1,256,1024]{2,1,0:T(8,128)S(1)} %collective-permute-done.4, f32[5,256,1024]{2,1,0:T(8,128)S(1)} %broadcast_multiply_fusion), kind=kLoop, calls=%fused_computation.15 | loop fusion | flops 1048576 | bytes 6291456 | tf_op jit(solution)/shard_map/add | solution.py:52
  (2 shorter events, 0.0 us)
Async XLA Ops:
  0.6 63.4 %copy-start = (f32[256,1024]{1,0:T(8,128)S(1)}, f32[256,1024]{1,0:T(8,128)}, u32[]{:S(2)}) copy-start(f32[256,1024]{1,0:T(8,128)} %param.4) | copy-start | bytes 3145732
  0.6 22.6 %collective-permute-start = (f32[1,256,1024]{2,1,0:T(8,128)}, f32[1,256,1024]{2,1,0:T(8,128)S(1)}, u32[]{:S(2)}, u32[]{:S(2)}) collective-permute-start(f32[1,256,1024]{2,1,0:T(8,128)} %bitcast.21), channel_id=1, source_target_pairs={{0,1},{1,2},{2,3},{3,4},{4,5},{5,6},{6,7},{7,0},{8,9},{9,10},{10,1... | collective-permute-start | bytes 3145736 | tf_op jit(solution)/shard_map/ppermute | solution.py:19
  4.6 59.2 %collective-permute-start.1 = (f32[1,256,1024]{2,1,0:T(8,128)}, f32[1,256,1024]{2,1,0:T(8,128)S(1)}, u32[]{:S(2)}, u32[]{:S(2)}) collective-permute-start(f32[1,256,1024]{2,1,0:T(8,128)} %bitcast.22), channel_id=1, source_target_pairs={{1,0},{2,1},{3,2},{4,3},{5,4},{6,5},{7,6},{0,7},{9,8},{10,9},{11,1... | collective-permute-start | bytes 3145736 | tf_op jit(solution)/shard_map/ppermute | solution.py:21
  6.5 57.3 %collective-permute-start.2 = (f32[1,256,1024]{2,1,0:T(8,128)}, f32[1,256,1024]{2,1,0:T(8,128)S(1)}, u32[]{:S(2)}, u32[]{:S(2)}) collective-permute-start(f32[1,256,1024]{2,1,0:T(8,128)} %bitcast.23), channel_id=1, source_target_pairs={{0,8},{8,16},{16,24},{24,32},{32,40},{40,48},{48,56},{56,64},{64,7... | collective-permute-start | bytes 3145736 | tf_op jit(solution)/shard_map/ppermute | solution.py:19
  8.4 55.5 %collective-permute-start.3 = (f32[1,256,1024]{2,1,0:T(8,128)}, f32[1,256,1024]{2,1,0:T(8,128)S(1)}, u32[]{:S(2)}, u32[]{:S(2)}) collective-permute-start(f32[1,256,1024]{2,1,0:T(8,128)} %bitcast.24), channel_id=1, source_target_pairs={{8,0},{16,8},{24,16},{32,24},{40,32},{48,40},{56,48},{64,56},{72,6... | collective-permute-start | bytes 3145736 | tf_op jit(solution)/shard_map/ppermute | solution.py:21
  64.0 4.4 %copy-start.1 = (s32[256]{0:T(256)S(1)}, s32[256]{0:T(256)}, u32[]{:S(2)}) copy-start(s32[256]{0:T(256)} %param.7) | copy-start | bytes 3076
  74.6 62.6 %collective-permute-start.7 = (f32[1,256,1024]{2,1,0:T(8,128)S(1)}, f32[1,256,1024]{2,1,0:T(8,128)S(1)}, u32[]{:S(2)}, u32[]{:S(2)}) collective-permute-start(f32[1,256,1024]{2,1,0:T(8,128)S(1)} %get-tuple-element.8), channel_id=1, source_target_pairs={{8,0},{16,8},{24,16},{32,24},{40,32},{48,40},{56,48},{64,56},{72,6... | collective-permute-start | bytes 3145736 | tf_op jit(solution)/shard_map/ppermute | solution.py:21
  76.5 60.6 %collective-permute-start.6 = (f32[1,256,1024]{2,1,0:T(8,128)S(1)}, f32[1,256,1024]{2,1,0:T(8,128)S(1)}, u32[]{:S(2)}, u32[]{:S(2)}) collective-permute-start(f32[1,256,1024]{2,1,0:T(8,128)S(1)} %get-tuple-element.9), channel_id=1, source_target_pairs={{0,8},{8,16},{16,24},{24,32},{32,40},{40,48},{48,56},{56,64},{64,7... | collective-permute-start | bytes 3145736 | tf_op jit(solution)/shard_map/ppermute | solution.py:19
  88.0 62.9 %collective-permute-start.5 = (f32[1,256,1024]{2,1,0:T(8,128)S(1)}, f32[1,256,1024]{2,1,0:T(8,128)S(1)}, u32[]{:S(2)}, u32[]{:S(2)}) collective-permute-start(f32[1,256,1024]{2,1,0:T(8,128)S(1)} %get-tuple-element.10), channel_id=1, source_target_pairs={{1,0},{2,1},{3,2},{4,3},{5,4},{6,5},{7,6},{0,7},{9,8},{10,9},{11,1... | collective-permute-start | bytes 3145736 | tf_op jit(solution)/shard_map/ppermute | solution.py:21
  89.9 61.0 %collective-permute-start.4 = (f32[1,256,1024]{2,1,0:T(8,128)S(1)}, f32[1,256,1024]{2,1,0:T(8,128)S(1)}, u32[]{:S(2)}, u32[]{:S(2)}) collective-permute-start(f32[1,256,1024]{2,1,0:T(8,128)S(1)} %get-tuple-element.7), channel_id=1, source_target_pairs={{0,1},{1,2},{2,3},{3,4},{4,5},{5,6},{6,7},{7,0},{8,9},{9,10},{10,1... | collective-permute-start | bytes 3145736 | tf_op jit(solution)/shard_map/ppermute | solution.py:19
where the time goes:
time: 153 us; the launch traced here: 152 us
  starting transfers between devices  67.8 us (44%)
  waiting for transfers between devices  63.7 us (42%)
  matrix products  14.8 us (10%)
  other arithmetic  3.26 us (2%)
  local copies, waits for them, and re-layouts  2.16 us (1%)
    ppermute x4, starting transfers between devices, with_halo(): lax.ppermute(tail, axis, [(i, (i + 1) % count) for i in range(ends)])  58.7 us
    ppermute x4, waiting for transfers between devices, with_halo(): lax.ppermute(head, axis, [((i + 1) % count, i) for i in range(ends)])  54.2 us
    ppermute x4, waiting for transfers between devices, with_halo(): lax.ppermute(tail, axis, [(i, (i + 1) % count) for i in range(ends)])  9.54 us
    ppermute x4, starting transfers between devices, with_halo(): lax.ppermute(head, axis, [((i + 1) % count, i) for i in range(ends)])  9.13 us
    dot_general x1, matrix products, local(): jnp.einsum('ioj,ojd->id', weights, stacked, precision=HIGH) * sharpness  5.85 us
    dot_general x1, matrix products, local(): jnp.einsum('ioj,id->ojd', weights, queries, precision=HIGH) * sharpness  4.56 us
    dot_general x1, matrix products, local(): jnp.einsum('id,ojd->ioj', queries, stacked, precision=HIGH) * sharpness  4.35 us
  transfers between devices with their start and end apart: 8, of which 3 were waited for; matrix products, arithmetic and copies ran while one was open for 5% of the time, Pallas kernels for 0%

commit v1 on v0

v1 whole, which is shorter than its diff:
```python
import functools
import math

import jax
import jax.numpy as jnp
from jax import lax
from jax.experimental import pallas as pl
from jax.experimental.pallas import tpu as pltpu
from jax.sharding import PartitionSpec as P

FULL = lax.Precision.HIGHEST
AXES = ("group", "loop")
BANDS, SECTORS, ZS = 64, 8, 8
SEAM = 31
FAR = 1e30
VMEM_BYTES = 40 * 1024 * 1024


def at(x, y, z, core):
    band = (y // 4) * 32 + x * ZS + z
    return band * SECTORS + (y % 4) * 2 + core


def seam_column(y, core, which):
    if (y % 4 >= 2) == (which == 1):
        return (3, 0) if core else (0, 7)
    if y < 4:
        return (2, 0) if core else (1, 0)
    return (1, 7) if core else (2, 7)


def seam_pairs(which):
    out, onward = [], []
    for y in range(8):
        for core in range(2):
            up = y < 4
            here = at(3, y, 7, core) if up else at(0, y, 0, core)
            there = at(0, y + 4, 0, core) if up else at(3, y - 4, 7, core)
            x, z = seam_column(y, core, which)
            relay = at(x, y, z, core)
            out.append((here, relay))
            onward.append((relay, there))
    return out, onward


def sector_swap(first):
    pairs = []
    for b in range(BANDS):
        for s in range(first, SECTORS + first, 2):
            i, j = b * SECTORS + s, b * SECTORS + (s + 1) % SECTORS
            pairs += [(i, j), (j, i)]
    return pairs


def band_pairs(b):
    pairs = []
    for s in range(SECTORS):
        i, j = b * SECTORS + s, (b + 1) * SECTORS + s
        pairs += [(i, j), (j, i)]
    return pairs


def band_swap(first):
    return sum([band_pairs(b) for b in range(first, BANDS - 1, 2) if b != SEAM], [])


def seam_swap():
    return band_pairs(SEAM)


def send(value, pairs):
    return lax.ppermute(value, AXES, pairs)


def outer(a, b):
    return lax.dot_general(a, b, (((1,), (1,)), ((), ())), precision=FULL, preferred_element_type=jnp.float32)


def inner(a, b):
    return jnp.dot(a, b, precision=FULL, preferred_element_type=jnp.float32)


def call(body, out, args, smem=0, later=(), flops=0, name=None):
    vmem = pl.BlockSpec(memory_space=pltpu.VMEM)
    scalar = pl.BlockSpec(memory_space=pltpu.SMEM)
    out = [a if isinstance(a, jax.ShapeDtypeStruct) else jax.ShapeDtypeStruct(a, jnp.float32) for a in out]
    moved = sum(a.dtype.itemsize * math.prod(a.shape) for a in list(args) + out)
    count = len(args) - smem
    args = list(args) + list(later)

    def run(*refs):
        body(*refs[:smem + count], *refs[len(args):])

    return pl.pallas_call(
        run,
        out_shape=out,
        in_specs=[scalar] * smem + [vmem] * count + [pl.BlockSpec(memory_space=pl.ANY)] * len(later),
        out_specs=[vmem] * len(out),
        compiler_params=pltpu.CompilerParams(vmem_limit_bytes=VMEM_BYTES),
        cost_estimate=pl.CostEstimate(flops=flops, bytes_accessed=moved, transcendentals=0),
        name=name,
    )(*args)


def mark(out):
    out[...] = jnp.zeros_like(out)


def after(*arrays):
    return call(mark, [(8, 128)], [], later=arrays, name="after")[0]


def passed(value, out):
    out[...] = value[...]


def first_scores(sharpness, q, k, ka, s0, sa):
    big = q[...] * sharpness
    s0[...] = outer(big, k[...])
    sa[...] = outer(big, ka[...])


def scores(sharpness, q, k, s):
    s[...] = outer(q[...] * sharpness, k[...])


def column(row):
    return jnp.broadcast_to(row, (128, row.shape[1])).T[:, :1]


def as_row(col):
    return jnp.broadcast_to(col, (col.shape[0], 128)).T[:1]


def softmax(sharpness, place, allowed, s0, sa, sb, sc, sd, seam, q, positive, weights, loss, aux, term_a, term_b):
    t = q.shape[0]
    for o, s in enumerate((s0, sa, sb, sc, sd)):
        weights[:, o * t:(o + 1) * t] = s[...]

    @pl.when(place[0] > 0)
    def _():
        weights[:, 4 * t:] = outer(q[...] * sharpness, seam[...])

    pick = column(positive[...])
    columns = lax.broadcasted_iota(jnp.int32, (t, t), 1)
    blocks = [weights[:, o * t:(o + 1) * t] for o in range(5)]
    masked = [jnp.where(allowed[place[1 + o]] > 0, b, -FAR) for o, b in enumerate(blocks)]
    highest = jnp.max(functools.reduce(jnp.maximum, masked), axis=1, keepdims=True)
    powers = [jnp.exp(m - highest) for m in masked]
    total = jnp.sum(sum(powers), axis=1, keepdims=True)
    log_total = highest + jnp.log(total)
    hits = [pick == columns + place[1 + o] * t for o in range(5)]
    score = sum(jnp.where(h, b, 0.0) for h, b in zip(hits, blocks))
    loss[...] = as_row(log_total - jnp.sum(score, axis=1, keepdims=True))
    share = sharpness / total
    for o, (p, h) in enumerate(zip(powers, hits)):
        weights[:, o * t:(o + 1) * t] = p * share - jnp.where(h, sharpness, 0.0)
    logs = as_row(log_total)
    aux[...] = jnp.zeros_like(aux)
    aux[0:1] = jnp.where(allowed[place[5]] > 0, logs, FAR)
    aux[1:2] = (positive[...] - place[5] * t).astype(jnp.float32)
    term_a[...] = inner(weights[:, t:2 * t].T, q[...])
    term_b[...] = inner(weights[:, 2 * t:3 * t].T, q[...])


def band_terms(weights, q, term_c, term_d):
    t = q.shape[0]
    term_c[...] = inner(weights[:, 3 * t:4 * t].T, q[...])
    term_d[...] = inner(weights[:, 4 * t:].T, q[...])


def query_gradient(place, weights, q, k, ka, kb, kc, kd, seam, gq, own):
    t = k.shape[0]
    own[...] = inner(weights[:, :t].T, q[...])
    weight = lambda o: weights[:, o * t:(o + 1) * t]
    total = inner(weight(0), k[...])
    for o, key in enumerate((ka, kb, kc)):
        total += inner(weight(o + 1), key[...])
    gq[...] = total

    @pl.when(place[0] > 0)
    def _():
        gq[...] += inner(weight(4), seam[...])

    @pl.when(place[0] == 0)
    def _():
        gq[...] += inner(weight(4), kd[...])


def key_sum(own, ta, tb, tc, td, out):
    out[...] = own[...] + ta[...] + tb[...] + tc[...] + td[...]


def seam_scores(sharpness, place, k, q, s):
    @pl.when(place[0] > 0)
    def _():
        s[...] = outer(k[...] * sharpness, q[...])


def key_gradient(sharpness, place, some, s, q, aux, gk):
    t = s.shape[0]
    gk[...] = some[...]

    @pl.when(place[0] > 0)
    def _():
        rows = lax.broadcasted_iota(jnp.int32, (t, t), 0)
        hits = rows == aux[1:2].astype(jnp.int32)
        w = (jnp.exp(s[...] - aux[0:1]) - jnp.where(hits, 1.0, 0.0)) * sharpness
        gk[...] += inner(w, q[...])


def local(queries, keys, pattern, positive):
    t, d = queries.shape
    sharpness = math.sqrt(d)
    one = 2 * t * t * d
    band, sector = lax.axis_index("group"), lax.axis_index("loop")
    odd_band, odd_sector = band % 2, sector % 2
    at_seam = (band == SEAM) | (band == SEAM + 1)
    place = jnp.stack([
        at_seam.astype(jnp.int32),
        0 * band,
        2 - odd_sector,
        1 + odd_sector,
        4 - odd_band,
        3 + odd_band,
    ])
    swap_a, swap_b = sector_swap(0), sector_swap(1)
    swap_c, swap_d = band_swap(0), band_swap(1)
    out_k, onward_k = seam_pairs(0)
    out_q, onward_q = seam_pairs(1)
    score = functools.partial(call, functools.partial(scores, sharpness), [(t, t)], flops=one)

    hop = send(keys, out_k)
    kb = send(keys, swap_b)
    kc = send(keys, swap_c)
    kd = send(keys, swap_d)
    ka = send(keys, swap_a)
    s0, sa = call(
        functools.partial(first_scores, sharpness),
        [(t, t), (t, t)],
        [queries, keys, ka], later=[hop], flops=2 * one, name="first_scores",
    )
    seam = send(hop, onward_k)
    hop_q = send(queries, out_q)
    (sb,) = score([queries, kb], later=[s0], name="scores_b")
    (sc,) = score([queries, kc], later=[sb], name="scores_c")
    (sd,) = score([queries, kd], later=[sc], name="scores_d")
    seam_q = send(hop_q, onward_q)
    weights, loss, aux, term_a, term_b = call(
        functools.partial(softmax, sharpness),
        [(t, 5 * t), (1, t), (8, t), (t, d), (t, d)],
        [place, pattern[0], s0, sa, sb, sc, sd, seam, queries, positive[None]],
        smem=2, later=[hop_q], flops=3 * one, name="softmax",
    )
    ta = send(term_a, swap_a)
    tb = send(term_b, swap_b)
    term_c, term_d = call(band_terms, [(t, d), (t, d)], [weights, queries], flops=2 * one, name="band_terms")
    tc = send(term_c, swap_c)
    td = send(term_d, swap_d)
    grad_queries, own = call(
        query_gradient,
        [(t, d), (t, d)],
        [place, weights, queries, keys, ka, kb, kc, kd, seam],
        smem=1, later=[term_c], flops=6 * one, name="query_gradient",
    )
    (aux,) = call(passed, [(8, t)], [aux], later=[grad_queries, ta], name="passed")
    aux_seam = send(aux, seam_swap())
    order = after(tb, aux_seam)
    order = after(tc, order)
    order = after(td, order)
    (some,) = call(key_sum, [(t, d)], [own, ta, tb, tc, td], later=[order], name="key_sum")
    (ss,) = call(functools.partial(seam_scores, sharpness), [(t, t)], [place, keys, seam_q], smem=1, later=[some], flops=one, name="seam_scores")
    (grad_keys,) = call(
        functools.partial(key_gradient, sharpness),
        [(t, d)],
        [place, some, ss, seam_q, aux_seam],
        smem=1, flops=one, name="key_gradient",
    )
    return loss[0], grad_queries, grad_keys


def solution(mesh):
    rows, flat = P(("loop", "group"), None), P(("loop", "group"))
    return jax.shard_map(
        local,
        mesh=mesh,
        in_specs=(rows, rows, rows, flat),
        out_specs=(flat, rows, rows),
        check_vma=False,
    )
```

time: 153 us -> 109 us (0.71)
  the two profiles are of different devices: /device:TPU:455 before, /device:TPU:59 now
where the time goes in v1:
time: 109 us
  starting transfers between devices  47.2 us (43%)
  waiting for transfers between devices  32.9 us (30%)
  Pallas kernels  21.7 us (20%)
  local copies, waits for them, and re-layouts  5.97 us (5%)
    ppermute x13, starting transfers between devices, send(): return lax.ppermute(value, AXES, pairs)  47.2 us
    ppermute x13, waiting for transfers between devices, send(): return lax.ppermute(value, AXES, pairs)  32.9 us
    pallas_call x14, Pallas kernels, call(): pl.pallas_call(run, out_shape=out, in_specs=[scalar] * smem + [vmem] * co...  21.7 us
    unnamed x18, local copies, waits for them, and re-layouts  5.89 us
  transfers between devices with their start and end apart: 13, of which 5 were waited for; matrix products, arithmetic and copies ran while one was open for 0% of the time, Pallas kernels for 14%

profile of v1, /device:TPU:59, one launch (start us, length us, event | category | flops | bytes accessed | tf_op | source)
XLA Modules:
  0.0 108.6 jit_solution(17907930207861489246)
XLA Ops:
  0.6 1.6 %collective-permute-start.1 = (f32[256,1024]{1,0:T(8,128)}, f32[256,1024]{1,0:T(8,128)}, u32[]{:S(2)}, u32[]{:S(2)}) collective-permute-start(f32[256,1024]{1,0:T(8,128)} %refs_1_.5), channel_id=1, source_target_pairs={{248,56},{249,193},{250,58},{251,195},{252,68},{253,133},{254,70},... | collective-permute-start | bytes 3145736 | tf_op jit(solution)/shard_map/ppermute | solution.py:72
  2.3 2.6 %collective-permute-start = (f32[256,1024]{1,0:T(8,128)}, f32[256,1024]{1,0:T(8,128)S(1)}, u32[]{:S(2)}, u32[]{:S(2)}) collective-permute-start(f32[256,1024]{1,0:T(8,128)} %refs_1_.5), channel_id=1, source_target_pairs={{0,1},{1,0},{2,3},{3,2},{4,5},{5,4},{6,7},{7,6},{8,9},{9,8},{10,11... | collective-permute-start | bytes 3145736 | tf_op jit(solution)/shard_map/ppermute | solution.py:72
  4.8 4.4 %collective-permute-start.2 = (f32[256,1024]{1,0:T(8,128)}, f32[256,1024]{1,0:T(8,128)S(1)}, u32[]{:S(2)}, u32[]{:S(2)}) collective-permute-start(f32[256,1024]{1,0:T(8,128)} %refs_1_.5), channel_id=1, source_target_pairs={{1,2},{2,1},{3,4},{4,3},{5,6},{6,5},{7,0},{0,7},{9,10},{10,9},{11,... | collective-permute-start | bytes 3145736 | tf_op jit(solution)/shard_map/ppermute | solution.py:72
  9.3 4.0 %collective-permute-start.3 = (f32[256,1024]{1,0:T(8,128)}, f32[256,1024]{1,0:T(8,128)S(1)}, u32[]{:S(2)}, u32[]{:S(2)}) collective-permute-start(f32[256,1024]{1,0:T(8,128)} %refs_1_.5), channel_id=1, source_target_pairs={{0,8},{8,0},{1,9},{9,1},{2,10},{10,2},{3,11},{11,3},{4,12},{12,4},... | collective-permute-start | bytes 3145736 | tf_op jit(solution)/shard_map/ppermute | solution.py:72
  13.3 8.8 %collective-permute-start.4 = (f32[256,1024]{1,0:T(8,128)}, f32[256,1024]{1,0:T(8,128)S(1)}, u32[]{:S(2)}, u32[]{:S(2)}) collective-permute-start(f32[256,1024]{1,0:T(8,128)} %refs_1_.5), channel_id=1, source_target_pairs={{8,16},{16,8},{9,17},{17,9},{10,18},{18,10},{11,19},{19,11},{12,20... | collective-permute-start | bytes 3145736 | tf_op jit(solution)/shard_map/ppermute | solution.py:72
  22.2 1.7 %collective-permute-start.6 = (f32[256,1024]{1,0:T(8,128)}, f32[256,1024]{1,0:T(8,128)}, u32[]{:S(2)}, u32[]{:S(2)}) collective-permute-start(f32[256,1024]{1,0:T(8,128)} %refs_2_.1), channel_id=1, source_target_pairs={{248,64},{249,129},{250,66},{251,131},{252,60},{253,197},{254,62},... | collective-permute-start | bytes 3145736 | tf_op jit(solution)/shard_map/ppermute | solution.py:72
  23.8 1.0 copy-done.3
  24.8 1.6 %collective-permute-start.5 = (f32[256,1024]{1,0:T(8,128)}, f32[256,1024]{1,0:T(8,128)}, u32[]{:S(2)}, u32[]{:S(2)}) collective-permute-start(f32[256,1024]{1,0:T(8,128)} %collective-permute-done.1.refs_3_), channel_id=1, source_target_pairs={{56,256},{193,257},{58,258},{195,259},{68,260},{133,261},{70,262},... | collective-permute-start | bytes 3145736 | tf_op jit(solution)/shard_map/ppermute | solution.py:72
  26.5 1.2 %copy-done = f32[256,1024]{1,0:T(8,128)S(1)} copy-done((f32[256,1024]{1,0:T(8,128)S(1)}, f32[256,1024]{1,0:T(8,128)}, u32[]{:S(2)}) %copy-start) | copy-done | bytes 1048600
  27.8 1.2 %copy-done.1 = f32[256,1024]{1,0:T(8,128)S(1)} copy-done((f32[256,1024]{1,0:T(8,128)S(1)}, f32[256,1024]{1,0:T(8,128)}, u32[]{:S(2)}) %copy-start.1) | copy-done | bytes 1048600
  29.0 1.2 %copy-done.4 = f32[256,1024]{1,0:T(8,128)S(1)} copy-done((f32[256,1024]{1,0:T(8,128)S(1)}, f32[256,1024]{1,0:T(8,128)}, u32[]{:S(2)}) %copy-start.4) | copy-done | bytes 1048600
  30.2 1.9 %first_scores.1 = (f32[256,256]{1,0:T(8,128)S(1)}, f32[256,256]{1,0:T(8,128)S(1)}) custom-call(f32[256,1024]{1,0:T(8,128)S(1)} %copy-done, f32[256,1024]{1,0:T(8,128)S(1)} %copy-done.1, f32[256,1024]{1,0:T(8,128)S(1)} %copy-done.4, f32[256,1024]{1,0:T(8,128)} %collective-permute-done.1.refs_3_), custom_call_target="tpu_custom_call" | custom-call | flops 268435456 | bytes 3670016 | tf_op jit(solution)/shard_map/first_scores/pallas_call | solution.py:94
  32.1 1.5 %collective-permute-done.2.refs_1_.refs_5_ = f32[256,1024]{1,0:T(8,128)S(1)} collective-permute-done((f32[256,1024]{1,0:T(8,128)}, f32[256,1024]{1,0:T(8,128)S(1)}, u32[]{:S(2)}, u32[]{:S(2)}) %collective-permute-start.2) | collective-permute-done | bytes 1048608 | tf_op jit(solution)/shard_map/ppermute | solution.py:72
  33.6 1.2 %scores_b.1.refs_2_.refs_4_ = f32[256,256]{1,0:T(8,128)S(1)} custom-call(f32[256,1024]{1,0:T(8,128)S(1)} %copy-done, f32[256,1024]{1,0:T(8,128)S(1)} %collective-permute-done.2.refs_1_.refs_5_, f32[256,256]{1,0:T(8,128)S(1)} %get-tuple-element.14.refs_2_), custom_call_target="tpu_custom_call" | custom-call | flops 134217728 | bytes 2359296 | tf_op jit(solution)/shard_map/scores_b/pallas_call | solution.py:94
  34.8 1.6 %collective-permute-done.3.refs_1_.refs_6_ = f32[256,1024]{1,0:T(8,128)S(1)} collective-permute-done((f32[256,1024]{1,0:T(8,128)}, f32[256,1024]{1,0:T(8,128)S(1)}, u32[]{:S(2)}, u32[]{:S(2)}) %collective-permute-start.3) | collective-permute-done | bytes 1048608 | tf_op jit(solution)/shard_map/ppermute | solution.py:72
  36.3 1.2 %scores_c.1.refs_2_.refs_5_ = f32[256,256]{1,0:T(8,128)S(1)} custom-call(f32[256,1024]{1,0:T(8,128)S(1)} %copy-done, f32[256,1024]{1,0:T(8,128)S(1)} %collective-permute-done.3.refs_1_.refs_6_, f32[256,256]{1,0:T(8,128)S(1)} %scores_b.1.refs_2_.refs_4_), custom_call_target="tpu_custom_call" | custom-call | flops 134217728 | bytes 2359296 | tf_op jit(solution)/shard_map/scores_c/pallas_call | solution.py:94
  37.5 7.6 %collective-permute-done.4.refs_1_.refs_7_ = f32[256,1024]{1,0:T(8,128)S(1)} collective-permute-done((f32[256,1024]{1,0:T(8,128)}, f32[256,1024]{1,0:T(8,128)S(1)}, u32[]{:S(2)}, u32[]{:S(2)}) %collective-permute-start.4) | collective-permute-done | bytes 1048608 | tf_op jit(solution)/shard_map/ppermute | solution.py:72
  45.1 1.2 %scores_d.1.refs_6_ = f32[256,256]{1,0:T(8,128)S(1)} custom-call(f32[256,1024]{1,0:T(8,128)S(1)} %copy-done, f32[256,1024]{1,0:T(8,128)S(1)} %collective-permute-done.4.refs_1_.refs_7_, f32[256,256]{1,0:T(8,128)S(1)} %scores_c.1.refs_2_.refs_5_), custom_call_target="tpu_custom_call" | custom-call | flops 134217728 | bytes 2359296 | tf_op jit(solution)/shard_map/scores_d/pallas_call | solution.py:94
  46.4 4.3 %softmax.1 = (f32[256,1280]{1,0:T(8,128)S(1)}, f32[1,256]{1,0:T(1,128)}, f32[8,256]{1,0:T(8,128)S(1)}, f32[256,1024]{1,0:T(8,128)S(1)}, f32[256,1024]{1,0:T(8,128)S(1)}) custom-call(s32[6]{0:T(128)S(1)} %stack.27.refs_0_, s32[5]{0:T(128)S(1)} %bitcast.9, f32[256,256]{1,0:T(8,128)S(1)} %get-tuple-element.14.refs_2_, ...), custom_call_target="tpu_custom_call" | custom-call | flops 402653184 | bytes 6826028 | tf_op jit(solution)/shard_map/softmax/pallas_call | solution.py:94
  50.7 2.2 %collective-permute-start.7 = (f32[256,1024]{1,0:T(8,128)S(1)}, f32[256,1024]{1,0:T(8,128)S(1)}, u32[]{:S(2)}, u32[]{:S(2)}) collective-permute-start(f32[256,1024]{1,0:T(8,128)S(1)} %get-tuple-element.21), channel_id=1, source_target_pairs={{0,1},{1,0},{2,3},{3,2},{4,5},{5,4},{6,7},{7,6},{8,9},{9,8},{10,11... | collective-permute-start | bytes 3145736 | tf_op jit(solution)/shard_map/ppermute | solution.py:72
  52.8 14.8 %collective-permute-start.8 = (f32[256,1024]{1,0:T(8,128)S(1)}, f32[256,1024]{1,0:T(8,128)S(1)}, u32[]{:S(2)}, u32[]{:S(2)}) collective-permute-start(f32[256,1024]{1,0:T(8,128)S(1)} %get-tuple-element.22), channel_id=1, source_target_pairs={{1,2},{2,1},{3,4},{4,3},{5,6},{6,5},{7,0},{0,7},{9,10},{10,9},{11,... | collective-permute-start | bytes 3145736 | tf_op jit(solution)/shard_map/ppermute | solution.py:72
  67.6 1.9 %band_terms.1 = (f32[256,1024]{1,0:T(8,128)S(1)}, f32[256,1024]{1,0:T(8,128)S(1)}) custom-call(f32[256,1280]{1,0:T(8,128)S(1)} %get-tuple-element.17.refs_0_.refs_1_, f32[256,1024]{1,0:T(8,128)S(1)} %copy-done), custom_call_target="tpu_custom_call" | custom-call | flops 268435456 | bytes 4456448 | tf_op jit(solution)/shard_map/band_terms/pallas_call | solution.py:94
  69.6 1.9 %collective-permute-start.9 = (f32[256,1024]{1,0:T(8,128)S(1)}, f32[256,1024]{1,0:T(8,128)S(1)}, u32[]{:S(2)}, u32[]{:S(2)}) collective-permute-start(f32[256,1024]{1,0:T(8,128)S(1)} %get-tuple-element.18.refs_9_), channel_id=1, source_target_pairs={{0,8},{8,0},{1,9},{9,1},{2,10},{10,2},{3,11},{11,3},{4,12},{12,4},... | collective-permute-start | bytes 3145736 | tf_op jit(solution)/shard_map/ppermute | solution.py:72
  71.5 2.1 %collective-permute-start.10 = (f32[256,1024]{1,0:T(8,128)S(1)}, f32[256,1024]{1,0:T(8,128)S(1)}, u32[]{:S(2)}, u32[]{:S(2)}) collective-permute-start(f32[256,1024]{1,0:T(8,128)S(1)} %get-tuple-element.23), channel_id=1, source_target_pairs={{8,16},{16,8},{9,17},{17,9},{10,18},{18,10},{11,19},{19,11},{12,20... | collective-permute-start | bytes 3145736 | tf_op jit(solution)/shard_map/ppermute | solution.py:72
  73.6 0.7 collective-permute-start.12
  74.4 7.7 %query_gradient.1 = (f32[256,1024]{1,0:T(8,128)}, f32[256,1024]{1,0:T(8,128)S(1)}) custom-call(s32[6]{0:T(128)S(1)} %stack.27.refs_0_, f32[256,1280]{1,0:T(8,128)S(1)} %get-tuple-element.17.refs_0_.refs_1_, f32[256,1024]{1,0:T(8,128)S(1)} %copy-done, f32[256,1024]{1,0:T(8,128)S(1)} %copy-done.2, f32[256,1024]{1,0:T(8,128)S(1)} %copy-done.5, ...), custom_call_target="tpu_custom_call" | custom-call | flops 805306368 | bytes 10747928 | tf_op jit(solution)/shard_map/query_gradient/pallas_call | solution.py:94
  82.1 1.2 %copy-done.6 = f32[256,1024]{1,0:T(8,128)S(1)} copy-done((f32[256,1024]{1,0:T(8,128)S(1)}, f32[256,1024]{1,0:T(8,128)}, u32[]{:S(2)}) %copy-start.6) | copy-done | bytes 1048600
  83.3 0.6 collective-permute-start.11
  84.0 7.1 %collective-permute-done.8.refs_0_.refs_2_ = f32[256,1024]{1,0:T(8,128)S(1)} collective-permute-done((f32[256,1024]{1,0:T(8,128)S(1)}, f32[256,1024]{1,0:T(8,128)S(1)}, u32[]{:S(2)}, u32[]{:S(2)}) %collective-permute-start.8) | collective-permute-done | bytes 1048608 | tf_op jit(solution)/shard_map/ppermute | solution.py:72
  91.1 15.1 %collective-permute-done.10.refs_0_.refs_4_ = f32[256,1024]{1,0:T(8,128)S(1)} collective-permute-done((f32[256,1024]{1,0:T(8,128)S(1)}, f32[256,1024]{1,0:T(8,128)S(1)}, u32[]{:S(2)}, u32[]{:S(2)}) %collective-permute-start.10) | collective-permute-done | bytes 1048608 | tf_op jit(solution)/shard_map/ppermute | solution.py:72
  106.4 0.6 seam_scores.1.refs_2_
  107.0 1.6 %key_gradient.1 = f32[256,1024]{1,0:T(8,128)} custom-call(s32[6]{0:T(128)S(1)} %stack.27.refs_0_, f32[256,1024]{1,0:T(8,128)S(1)} %key_sum.1.refs_3_.refs_1_, f32[256,256]{1,0:T(8,128)S(1)} %seam_scores.1.refs_2_, f32[256,1024]{1,0:T(8,128)S(1)} %collective-permute-done.12.refs_2_.refs_3_, f32[8,256]{1,0:T(8,128)S(1)} %collective-permute-done.11.refs_1_.refs_4_), custom_call_target="tpu_custom_call" | custom-call | flops 134217728 | bytes 3416088 | tf_op jit(solution)/shard_map/key_gradient/pallas_call | solution.py:94
  (27 shorter events, 0.4 us)
Async XLA Ops:
  0.6 21.5 %collective-permute-start.1 = (f32[256,1024]{1,0:T(8,128)}, f32[256,1024]{1,0:T(8,128)}, u32[]{:S(2)}, u32[]{:S(2)}) collective-permute-start(f32[256,1024]{1,0:T(8,128)} %refs_1_.5), channel_id=1, source_target_pairs={{248,56},{249,193},{250,58},{251,195},{252,68},{253,133},{254,70},... | collective-permute-start | bytes 3145736 | tf_op jit(solution)/shard_map/ppermute | solution.py:72
  2.3 21.6 %collective-permute-start = (f32[256,1024]{1,0:T(8,128)}, f32[256,1024]{1,0:T(8,128)S(1)}, u32[]{:S(2)}, u32[]{:S(2)}) collective-permute-start(f32[256,1024]{1,0:T(8,128)} %refs_1_.5), channel_id=1, source_target_pairs={{0,1},{1,0},{2,3},{3,2},{4,5},{5,4},{6,7},{7,6},{8,9},{9,8},{10,11... | collective-permute-start | bytes 3145736 | tf_op jit(solution)/shard_map/ppermute | solution.py:72
  4.8 28.8 %collective-permute-start.2 = (f32[256,1024]{1,0:T(8,128)}, f32[256,1024]{1,0:T(8,128)S(1)}, u32[]{:S(2)}, u32[]{:S(2)}) collective-permute-start(f32[256,1024]{1,0:T(8,128)} %refs_1_.5), channel_id=1, source_target_pairs={{1,2},{2,1},{3,4},{4,3},{5,6},{6,5},{7,0},{0,7},{9,10},{10,9},{11,... | collective-permute-start | bytes 3145736 | tf_op jit(solution)/shard_map/ppermute | solution.py:72
  9.3 27.0 %collective-permute-start.3 = (f32[256,1024]{1,0:T(8,128)}, f32[256,1024]{1,0:T(8,128)S(1)}, u32[]{:S(2)}, u32[]{:S(2)}) collective-permute-start(f32[256,1024]{1,0:T(8,128)} %refs_1_.5), channel_id=1, source_target_pairs={{0,8},{8,0},{1,9},{9,1},{2,10},{10,2},{3,11},{11,3},{4,12},{12,4},... | collective-permute-start | bytes 3145736 | tf_op jit(solution)/shard_map/ppermute | solution.py:72
  13.3 31.8 %collective-permute-start.4 = (f32[256,1024]{1,0:T(8,128)}, f32[256,1024]{1,0:T(8,128)S(1)}, u32[]{:S(2)}, u32[]{:S(2)}) collective-permute-start(f32[256,1024]{1,0:T(8,128)} %refs_1_.5), channel_id=1, source_target_pairs={{8,16},{16,8},{9,17},{17,9},{10,18},{18,10},{11,19},{19,11},{12,20... | collective-permute-start | bytes 3145736 | tf_op jit(solution)/shard_map/ppermute | solution.py:72
  22.2 24.2 %collective-permute-start.6 = (f32[256,1024]{1,0:T(8,128)}, f32[256,1024]{1,0:T(8,128)}, u32[]{:S(2)}, u32[]{:S(2)}) collective-permute-start(f32[256,1024]{1,0:T(8,128)} %refs_2_.1), channel_id=1, source_target_pairs={{248,64},{249,129},{250,66},{251,131},{252,60},{253,197},{254,62},... | collective-permute-start | bytes 3145736 | tf_op jit(solution)/shard_map/ppermute | solution.py:72
  23.8 1.0 copy-start.3
  24.8 21.5 %collective-permute-start.5 = (f32[256,1024]{1,0:T(8,128)}, f32[256,1024]{1,0:T(8,128)}, u32[]{:S(2)}, u32[]{:S(2)}) collective-permute-start(f32[256,1024]{1,0:T(8,128)} %collective-permute-done.1.refs_3_), channel_id=1, source_target_pairs={{56,256},{193,257},{58,258},{195,259},{68,260},{133,261},{70,262},... | collective-permute-start | bytes 3145736 | tf_op jit(solution)/shard_map/ppermute | solution.py:72
  26.5 1.2 %copy-start = (f32[256,1024]{1,0:T(8,128)S(1)}, f32[256,1024]{1,0:T(8,128)}, u32[]{:S(2)}) copy-start(f32[256,1024]{1,0:T(8,128)} %refs_2_.1) | copy-start | bytes 3145732
  27.8 1.2 %copy-start.1 = (f32[256,1024]{1,0:T(8,128)S(1)}, f32[256,1024]{1,0:T(8,128)}, u32[]{:S(2)}) copy-start(f32[256,1024]{1,0:T(8,128)} %refs_1_.5) | copy-start | bytes 3145732
  29.0 1.2 %copy-start.4 = (f32[256,1024]{1,0:T(8,128)S(1)}, f32[256,1024]{1,0:T(8,128)}, u32[]{:S(2)}) copy-start(f32[256,1024]{1,0:T(8,128)} %copy-done.3) | copy-start | bytes 3145732
  37.5 8.8 %copy-start.7 = (s32[256]{0:T(256)S(1)}, s32[256]{0:T(256)}, u32[]{:S(2)}) copy-start(s32[256]{0:T(256)} %param.7) | copy-start | bytes 3076
  37.5 8.8 %copy-start.8 = (s32[1,5]{1,0:T(1,128)S(1)}, s32[1,5]{1,0:T(1,128)}, u32[]{:S(2)}) copy-start(s32[1,5]{1,0:T(1,128)} %param.6) | copy-start | bytes 64
  50.7 23.7 %copy-start.2 = (f32[256,1024]{1,0:T(8,128)S(1)}, f32[256,1024]{1,0:T(8,128)}, u32[]{:S(2)}) copy-start(f32[256,1024]{1,0:T(8,128)} %refs_1_.5) | copy-start | bytes 3145732
  50.7 23.7 %copy-start.5 = (f32[256,1024]{1,0:T(8,128)S(1)}, f32[256,1024]{1,0:T(8,128)}, u32[]{:S(2)}) copy-start(f32[256,1024]{1,0:T(8,128)} %copy-done.3) | copy-start | bytes 3145732
  50.7 31.4 %collective-permute-start.7 = (f32[256,1024]{1,0:T(8,128)S(1)}, f32[256,1024]{1,0:T(8,128)S(1)}, u32[]{:S(2)}, u32[]{:S(2)}) collective-permute-start(f32[256,1024]{1,0:T(8,128)S(1)} %get-tuple-element.21), channel_id=1, source_target_pairs={{0,1},{1,0},{2,3},{3,2},{4,5},{5,4},{6,7},{7,6},{8,9},{9,8},{10,11... | collective-permute-start | bytes 3145736 | tf_op jit(solution)/shard_map/ppermute | solution.py:72
  52.8 38.2 %collective-permute-start.8 = (f32[256,1024]{1,0:T(8,128)S(1)}, f32[256,1024]{1,0:T(8,128)S(1)}, u32[]{:S(2)}, u32[]{:S(2)}) collective-permute-start(f32[256,1024]{1,0:T(8,128)S(1)} %get-tuple-element.22), channel_id=1, source_target_pairs={{1,2},{2,1},{3,4},{4,3},{5,6},{6,5},{7,0},{0,7},{9,10},{10,9},{11,... | collective-permute-start | bytes 3145736 | tf_op jit(solution)/shard_map/ppermute | solution.py:72
  69.6 21.5 %collective-permute-start.9 = (f32[256,1024]{1,0:T(8,128)S(1)}, f32[256,1024]{1,0:T(8,128)S(1)}, u32[]{:S(2)}, u32[]{:S(2)}) collective-permute-start(f32[256,1024]{1,0:T(8,128)S(1)} %get-tuple-element.18.refs_9_), channel_id=1, source_target_pairs={{0,8},{8,0},{1,9},{9,1},{2,10},{10,2},{3,11},{11,3},{4,12},{12,4},... | collective-permute-start | bytes 3145736 | tf_op jit(solution)/shard_map/ppermute | solution.py:72
  71.5 34.7 %collective-permute-start.10 = (f32[256,1024]{1,0:T(8,128)S(1)}, f32[256,1024]{1,0:T(8,128)S(1)}, u32[]{:S(2)}, u32[]{:S(2)}) collective-permute-start(f32[256,1024]{1,0:T(8,128)S(1)} %get-tuple-element.23), channel_id=1, source_target_pairs={{8,16},{16,8},{9,17},{17,9},{10,18},{18,10},{11,19},{19,11},{12,20... | collective-permute-start | bytes 3145736 | tf_op jit(solution)/shard_map/ppermute | solution.py:72
  73.6 32.8 %collective-permute-start.12 = (f32[256,1024]{1,0:T(8,128)}, f32[256,1024]{1,0:T(8,128)S(1)}, u32[]{:S(2)}, u32[]{:S(2)}) collective-permute-start(f32[256,1024]{1,0:T(8,128)} %collective-permute-done.6.refs_10_), channel_id=1, source_target_pairs={{64,256},{129,257},{66,258},{131,259},{60,260},{197,261},{62,262},... | collective-permute-start | bytes 3145736 | tf_op jit(solution)/shard_map/ppermute | solution.py:72
  82.1 1.2 %copy-start.6 = (f32[256,1024]{1,0:T(8,128)S(1)}, f32[256,1024]{1,0:T(8,128)}, u32[]{:S(2)}) copy-start(f32[256,1024]{1,0:T(8,128)} %get-tuple-element.12.refs_1_) | copy-start | bytes 3145732
  83.3 7.7 %collective-permute-start.11 = (f32[8,256]{1,0:T(8,128)S(1)}, f32[8,256]{1,0:T(8,128)S(1)}, u32[]{:S(2)}, u32[]{:S(2)}) collective-permute-start(f32[8,256]{1,0:T(8,128)S(1)} %passed.1), channel_id=1, source_target_pairs={{248,256},{256,248},{249,257},{257,249},{250,258},{258,250},{251,2... | collective-permute-start | bytes 24584 | tf_op jit(solution)/shard_map/ppermute | solution.py:72

commit v2 on v1

--- a/solution.py
+++ b/solution.py
@@ -13,7 +13,7 @@
 BANDS, SECTORS, ZS = 64, 8, 8
 SEAM = 31
 FAR = 1e30
-VMEM_BYTES = 40 * 1024 * 1024
+VMEM_BYTES = 24 * 1024 * 1024
 
 
 def at(x, y, z, core):
@@ -24,9 +24,9 @@
 def seam_column(y, core, which):
     if (y % 4 >= 2) == (which == 1):
         return (3, 0) if core else (0, 7)
-    if y < 4:
-        return (2, 0) if core else (1, 0)
-    return (1, 7) if core else (2, 7)
+    if which == 0:
+        return ((3, 0) if core else (1, 0)) if y < 4 else ((0, 0) if core else (2, 7))
+    return (1 + core, 0) if y < 4 else (2 - core, 7)
 
 
 def seam_pairs(which):
@@ -122,6 +122,11 @@
 
 def scores(sharpness, q, k, s):
     s[...] = outer(q[...] * sharpness, k[...])
+
+
+def scores_and_copy(sharpness, q, k, s, sent):
+    s[...] = outer(q[...] * sharpness, k[...])
+    sent[...] = q[...]
 
 
 def column(row):
@@ -157,16 +162,11 @@
         weights[:, o * t:(o + 1) * t] = p * share - jnp.where(h, sharpness, 0.0)
     logs = as_row(log_total)
     aux[...] = jnp.zeros_like(aux)
-    aux[0:1] = jnp.where(allowed[place[5]] > 0, logs, FAR)
-    aux[1:2] = (positive[...] - place[5] * t).astype(jnp.float32)
+    for o in range(5):
+        aux[o:o + 1] = jnp.where(allowed[o] > 0, logs, FAR)
+    aux[5:6] = positive[...].astype(jnp.float32)
+    term_b[...] = inner(weights[:, 2 * t:3 * t].T, q[...])
     term_a[...] = inner(weights[:, t:2 * t].T, q[...])
-    term_b[...] = inner(weights[:, 2 * t:3 * t].T, q[...])
-
-
-def band_terms(weights, q, term_c, term_d):
-    t = q.shape[0]
-    term_c[...] = inner(weights[:, 3 * t:4 * t].T, q[...])
-    term_d[...] = inner(weights[:, 4 * t:].T, q[...])
 
 
 def query_gradient(place, weights, q, k, ka, kb, kc, kd, seam, gq, own):
@@ -187,26 +187,46 @@
         gq[...] += inner(weight(4), kd[...])
 
 
-def key_sum(own, ta, tb, tc, td, out):
-    out[...] = own[...] + ta[...] + tb[...] + tc[...] + td[...]
-
-
-def seam_scores(sharpness, place, k, q, s):
+def seam_or(sharpness, place, k, q, seam, s):
     @pl.when(place[0] > 0)
     def _():
+        s[...] = outer(k[...] * sharpness, seam[...])
+
+    @pl.when(place[0] == 0)
+    def _():
         s[...] = outer(k[...] * sharpness, q[...])
 
 
-def key_gradient(sharpness, place, some, s, q, aux, gk):
+def key_weights(sharpness, slot, s, aux):
     t = s.shape[0]
-    gk[...] = some[...]
+    back = jnp.where(slot % 2 == 1, slot + 1, slot - 1)
+    logs = aux[1:2]
+    for o in range(2, 5):
+        logs = jnp.where(back == o, aux[o:o + 1], logs)
+    rows = lax.broadcasted_iota(jnp.int32, (t, t), 0) + back * t
+    hits = rows == aux[5:6].astype(jnp.int32)
+    return (jnp.exp(s[...] - logs) - jnp.where(hits, 1.0, 0.0)) * sharpness
+
+
+def keys_c(sharpness, place, own, ta, tc, qc, aux, out):
+    total = own[...] + ta[...]
+    out[...] = total + inner(key_weights(sharpness, place[4], tc, aux), qc[...])
+
+
+def keys_d(sharpness, place, some, td, qd, seam, aux, out):
+    w = key_weights(sharpness, place[5], td, aux)
 
     @pl.when(place[0] > 0)
     def _():
-        rows = lax.broadcasted_iota(jnp.int32, (t, t), 0)
-        hits = rows == aux[1:2].astype(jnp.int32)
-        w = (jnp.exp(s[...] - aux[0:1]) - jnp.where(hits, 1.0, 0.0)) * sharpness
-        gk[...] += inner(w, q[...])
+        out[...] = some[...] + inner(w, seam[...])
+
+    @pl.when(place[0] == 0)
+    def _():
+        out[...] = some[...] + inner(w, qd[...])
+
+
+def key_sum(some, tb, out):
+    out[...] = some[...] + tb[...]
 
 
 def local(queries, keys, pattern, positive):
@@ -242,7 +262,12 @@
     )
     seam = send(hop, onward_k)
     hop_q = send(queries, out_q)
-    (sb,) = score([queries, kb], later=[s0], name="scores_b")
+    sb, sent = call(
+        functools.partial(scores_and_copy, sharpness), [(t, t), (t, d)],
+        [queries, kb], later=[s0], flops=one, name="scores_b",
+    )
+    qc = send(sent, swap_c)
+    qd = send(sent, swap_d)
     (sc,) = score([queries, kc], later=[sb], name="scores_c")
     (sd,) = score([queries, kd], later=[sc], name="scores_d")
     seam_q = send(hop_q, onward_q)
@@ -252,30 +277,30 @@
         [place, pattern[0], s0, sa, sb, sc, sd, seam, queries, positive[None]],
         smem=2, later=[hop_q], flops=3 * one, name="softmax",
     )
-    ta = send(term_a, swap_a)
-    tb = send(term_b, swap_b)
-    term_c, term_d = call(band_terms, [(t, d), (t, d)], [weights, queries], flops=2 * one, name="band_terms")
-    tc = send(term_c, swap_c)
-    td = send(term_d, swap_d)
     grad_queries, own = call(
         query_gradient,
         [(t, d), (t, d)],
         [place, weights, queries, keys, ka, kb, kc, kd, seam],
-        smem=1, later=[term_c], flops=6 * one, name="query_gradient",
-    )
-    (aux,) = call(passed, [(8, t)], [aux], later=[grad_queries, ta], name="passed")
-    aux_seam = send(aux, seam_swap())
-    order = after(tb, aux_seam)
-    order = after(tc, order)
-    order = after(td, order)
-    (some,) = call(key_sum, [(t, d)], [own, ta, tb, tc, td], later=[order], name="key_sum")
-    (ss,) = call(functools.partial(seam_scores, sharpness), [(t, t)], [place, keys, seam_q], smem=1, later=[some], flops=one, name="seam_scores")
-    (grad_keys,) = call(
-        functools.partial(key_gradient, sharpness),
-        [(t, d)],
-        [place, some, ss, seam_q, aux_seam],
-        smem=1, flops=one, name="key_gradient",
-    )
+        smem=1, flops=6 * one, name="query_gradient",
+    )
+    (tc,) = score([keys, qc], later=[own], name="back_c")
+    tb = send(term_b, swap_b)
+    ta = send(term_a, swap_a)
+    aux_c = send(aux, swap_c)
+    aux_d = send(aux, swap_d + seam_swap())
+    (td,) = call(
+        functools.partial(seam_or, sharpness), [(t, t)],
+        [place, keys, qd, seam_q], smem=1, later=[tc], flops=one, name="back_d",
+    )
+    (some,) = call(
+        functools.partial(keys_c, sharpness), [(t, d)],
+        [place, own, ta, tc, qc, aux_c], smem=1, later=[td], flops=one, name="keys_c",
+    )
+    (some,) = call(
+        functools.partial(keys_d, sharpness), [(t, d)],
+        [place, some, td, qd, seam_q, aux_d], smem=1, flops=one, name="keys_d",
+    )
+    (grad_keys,) = call(key_sum, [(t, d)], [some, tb], name="key_sum")
     return loss[0], grad_queries, grad_keys
 
 

time: 109 us -> 104 us (0.954)
  the two profiles are of different devices: /device:TPU:59 before, /device:TPU:49 now
where the time goes in v2:
time: 104 us; the launch traced here: 103 us
  starting transfers between devices  60.4 us (58%)
  Pallas kernels  26.2 us (25%)
  waiting for transfers between devices  10.5 us (10%)
  local copies, waits for them, and re-layouts  4.75 us (5%)
    ppermute x14, starting transfers between devices, send(): return lax.ppermute(value, AXES, pairs)  60.4 us
    pallas_call x11, Pallas kernels, call(): pl.pallas_call(run, out_shape=out, in_specs=[scalar] * smem + [vmem] * co...  26.2 us
    ppermute x14, waiting for transfers between devices, send(): return lax.ppermute(value, AXES, pairs)  10.5 us
    unnamed x16, local copies, waits for them, and re-layouts  4.67 us
  transfers between devices with their start and end apart: 14, of which 2 were waited for; matrix products, arithmetic and copies ran while one was open for 0% of the time, Pallas kernels for 24%

profile of v2, /device:TPU:49, one launch (start us, length us, event | category | flops | bytes accessed | tf_op | source)
XLA Modules:
  0.0 102.8 jit_solution(15748782532256070613)
XLA Ops:
  0.6 2.6 %collective-permute-start = (f32[256,1024]{1,0:T(8,128)}, f32[256,1024]{1,0:T(8,128)S(1)}, u32[]{:S(2)}, u32[]{:S(2)}) collective-permute-start(f32[256,1024]{1,0:T(8,128)} %refs_1_.3), channel_id=1, source_target_pairs={{0,1},{1,0},{2,3},{3,2},{4,5},{5,4},{6,7},{7,6},{8,9},{9,8},{10,11... | collective-permute-start | bytes 3145736 | tf_op jit(solution)/shard_map/ppermute | solution.py:72
  3.2 9.4 %collective-permute-start.1 = (f32[256,1024]{1,0:T(8,128)}, f32[256,1024]{1,0:T(8,128)}, u32[]{:S(2)}, u32[]{:S(2)}) collective-permute-start(f32[256,1024]{1,0:T(8,128)} %refs_1_.3), channel_id=1, source_target_pairs={{248,56},{249,193},{250,58},{251,195},{252,68},{253,197},{254,70},... | collective-permute-start | bytes 3145736 | tf_op jit(solution)/shard_map/ppermute | solution.py:72
  12.7 7.1 %collective-permute-start.2 = (f32[256,1024]{1,0:T(8,128)}, f32[256,1024]{1,0:T(8,128)S(1)}, u32[]{:S(2)}, u32[]{:S(2)}) collective-permute-start(f32[256,1024]{1,0:T(8,128)} %refs_1_.3), channel_id=1, source_target_pairs={{1,2},{2,1},{3,4},{4,3},{5,6},{6,5},{7,0},{0,7},{9,10},{10,9},{11,... | collective-permute-start | bytes 3145736 | tf_op jit(solution)/shard_map/ppermute | solution.py:72
  19.8 1.9 %collective-permute-start.3 = (f32[256,1024]{1,0:T(8,128)}, f32[256,1024]{1,0:T(8,128)S(1)}, u32[]{:S(2)}, u32[]{:S(2)}) collective-permute-start(f32[256,1024]{1,0:T(8,128)} %refs_1_.3), channel_id=1, source_target_pairs={{0,8},{8,0},{1,9},{9,1},{2,10},{10,2},{3,11},{11,3},{4,12},{12,4},... | collective-permute-start | bytes 3145736 | tf_op jit(solution)/shard_map/ppermute | solution.py:72
  21.7 2.3 %collective-permute-start.6 = (f32[256,1024]{1,0:T(8,128)}, f32[256,1024]{1,0:T(8,128)}, u32[]{:S(2)}, u32[]{:S(2)}) collective-permute-start(f32[256,1024]{1,0:T(8,128)} %refs_2_.1), channel_id=1, source_target_pairs={{248,64},{249,129},{250,66},{251,131},{252,60},{253,197},{254,62},... | collective-permute-start | bytes 3145736 | tf_op jit(solution)/shard_map/ppermute | solution.py:72
  24.0 1.0 copy-done.3
  25.0 0.7 collective-permute-start.4
  25.8 16.0 %collective-permute-start.5 = (f32[256,1024]{1,0:T(8,128)}, f32[256,1024]{1,0:T(8,128)}, u32[]{:S(2)}, u32[]{:S(2)}) collective-permute-start(f32[256,1024]{1,0:T(8,128)} %collective-permute-done.1.refs_3_), channel_id=1, source_target_pairs={{56,256},{193,257},{58,258},{195,259},{68,260},{197,261},{70,262},... | collective-permute-start | bytes 3145736 | tf_op jit(solution)/shard_map/ppermute | solution.py:72
  41.8 0.1 stack.27.refs_0_
  41.9 1.2 %copy-done = f32[256,1024]{1,0:T(8,128)S(1)} copy-done((f32[256,1024]{1,0:T(8,128)S(1)}, f32[256,1024]{1,0:T(8,128)}, u32[]{:S(2)}) %copy-start) | copy-done | bytes 1048600
  43.1 1.2 %copy-done.1 = f32[256,1024]{1,0:T(8,128)S(1)} copy-done((f32[256,1024]{1,0:T(8,128)S(1)}, f32[256,1024]{1,0:T(8,128)}, u32[]{:S(2)}) %copy-start.1) | copy-done | bytes 1048600
  44.4 1.2 %copy-done.4 = f32[256,1024]{1,0:T(8,128)S(1)} copy-done((f32[256,1024]{1,0:T(8,128)S(1)}, f32[256,1024]{1,0:T(8,128)}, u32[]{:S(2)}) %copy-start.4) | copy-done | bytes 1048600
  45.6 1.9 %first_scores.1 = (f32[256,256]{1,0:T(8,128)S(1)}, f32[256,256]{1,0:T(8,128)S(1)}) custom-call(f32[256,1024]{1,0:T(8,128)S(1)} %copy-done, f32[256,1024]{1,0:T(8,128)S(1)} %copy-done.1, f32[256,1024]{1,0:T(8,128)S(1)} %copy-done.4, f32[256,1024]{1,0:T(8,128)} %collective-permute-done.1.refs_3_), custom_call_target="tpu_custom_call" | custom-call | flops 268435456 | bytes 3670016 | tf_op jit(solution)/shard_map/first_scores/pallas_call | solution.py:94
  47.5 1.2 %scores_b.1 = (f32[256,256]{1,0:T(8,128)S(1)}, f32[256,1024]{1,0:T(8,128)S(1)}) custom-call(f32[256,1024]{1,0:T(8,128)S(1)} %copy-done, f32[256,1024]{1,0:T(8,128)S(1)} %collective-permute-done.2.refs_1_.refs_5_, f32[256,256]{1,0:T(8,128)S(1)} %get-tuple-element.14.refs_2_), custom_call_target="tpu_custom_call" | custom-call | flops 134217728 | bytes 3407872 | tf_op jit(solution)/shard_map/scores_b/pallas_call | solution.py:94
  48.7 1.9 %collective-permute-start.8 = (f32[256,1024]{1,0:T(8,128)S(1)}, f32[256,1024]{1,0:T(8,128)S(1)}, u32[]{:S(2)}, u32[]{:S(2)}) collective-permute-start(f32[256,1024]{1,0:T(8,128)S(1)} %get-tuple-element.22), channel_id=1, source_target_pairs={{0,8},{8,0},{1,9},{9,1},{2,10},{10,2},{3,11},{11,3},{4,12},{12,4},... | collective-permute-start | bytes 3145736 | tf_op jit(solution)/shard_map/ppermute | solution.py:72
  50.6 0.7 collective-permute-start.10
  51.4 1.3 %collective-permute-start.11 = (f32[256,1024]{1,0:T(8,128)}, f32[256,1024]{1,0:T(8,128)S(1)}, u32[]{:S(2)}, u32[]{:S(2)}) collective-permute-start(f32[256,1024]{1,0:T(8,128)} %collective-permute-done.6.refs_10_), channel_id=1, source_target_pairs={{64,256},{129,257},{66,258},{131,259},{60,260},{197,261},{62,262},... | collective-permute-start | bytes 3145736 | tf_op jit(solution)/shard_map/ppermute | solution.py:72
  52.7 1.2 %scores_c.1.refs_2_.refs_5_ = f32[256,256]{1,0:T(8,128)S(1)} custom-call(f32[256,1024]{1,0:T(8,128)S(1)} %copy-done, f32[256,1024]{1,0:T(8,128)S(1)} %collective-permute-done.3.refs_1_.refs_6_, f32[256,256]{1,0:T(8,128)S(1)} %get-tuple-element.16.refs_2_.refs_4_), custom_call_target="tpu_custom_call" | custom-call | flops 134217728 | bytes 2359296 | tf_op jit(solution)/shard_map/scores_c/pallas_call | solution.py:94
  53.9 1.2 %scores_d.1.refs_6_ = f32[256,256]{1,0:T(8,128)S(1)} custom-call(f32[256,1024]{1,0:T(8,128)S(1)} %copy-done, f32[256,1024]{1,0:T(8,128)S(1)} %collective-permute-done.4.refs_1_.refs_7_, f32[256,256]{1,0:T(8,128)S(1)} %scores_c.1.refs_2_.refs_5_), custom_call_target="tpu_custom_call" | custom-call | flops 134217728 | bytes 2359296 | tf_op jit(solution)/shard_map/scores_d/pallas_call | solution.py:94
  55.0 3.2 %collective-permute-done.5.refs_7_.refs_8_ = f32[256,1024]{1,0:T(8,128)} collective-permute-done((f32[256,1024]{1,0:T(8,128)}, f32[256,1024]{1,0:T(8,128)}, u32[]{:S(2)}, u32[]{:S(2)}) %collective-permute-start.5) | collective-permute-done | bytes 1048608 | tf_op jit(solution)/shard_map/ppermute | solution.py:72
  58.3 5.6 %softmax.1 = (f32[256,1280]{1,0:T(8,128)S(1)}, f32[1,256]{1,0:T(1,128)}, f32[8,256]{1,0:T(8,128)S(1)}, f32[256,1024]{1,0:T(8,128)S(1)}, f32[256,1024]{1,0:T(8,128)S(1)}) custom-call(s32[6]{0:T(128)S(1)} %stack.27.refs_0_, s32[5]{0:T(128)S(1)} %bitcast.9, f32[256,256]{1,0:T(8,128)S(1)} %get-tuple-element.14.refs_2_, ...), custom_call_target="tpu_custom_call" | custom-call | flops 402653184 | bytes 6826028 | tf_op jit(solution)/shard_map/softmax/pallas_call | solution.py:94
  63.9 1.9 %collective-permute-start.7 = (f32[256,1024]{1,0:T(8,128)S(1)}, f32[256,1024]{1,0:T(8,128)S(1)}, u32[]{:S(2)}, u32[]{:S(2)}) collective-permute-start(f32[256,1024]{1,0:T(8,128)S(1)} %get-tuple-element.21), channel_id=1, source_target_pairs={{0,1},{1,0},{2,3},{3,2},{4,5},{5,4},{6,7},{7,6},{8,9},{9,8},{10,11... | collective-permute-start | bytes 3145736 | tf_op jit(solution)/shard_map/ppermute | solution.py:72
  65.8 7.0 %collective-permute-start.13 = (f32[256,1024]{1,0:T(8,128)S(1)}, f32[256,1024]{1,0:T(8,128)S(1)}, u32[]{:S(2)}, u32[]{:S(2)}) collective-permute-start(f32[256,1024]{1,0:T(8,128)S(1)} %get-tuple-element.24), channel_id=1, source_target_pairs={{1,2},{2,1},{3,4},{4,3},{5,6},{6,5},{7,0},{0,7},{9,10},{10,9},{11,... | collective-permute-start | bytes 3145736 | tf_op jit(solution)/shard_map/ppermute | solution.py:72
  72.8 7.8 %query_gradient.1 = (f32[256,1024]{1,0:T(8,128)}, f32[256,1024]{1,0:T(8,128)S(1)}) custom-call(s32[6]{0:T(128)S(1)} %stack.27.refs_0_, f32[256,1280]{1,0:T(8,128)S(1)} %get-tuple-element.18.refs_1_, f32[256,1024]{1,0:T(8,128)S(1)} %copy-done, f32[256,1024]{1,0:T(8,128)S(1)} %copy-done.2, f32[256,1024]{1,0:T(8,128)S(1)} %copy-done.5, ...), custom_call_target="tpu_custom_call" | custom-call | flops 805306368 | bytes 10747928 | tf_op jit(solution)/shard_map/query_gradient/pallas_call | solution.py:94
  80.6 1.9 %collective-permute-start.9 = (f32[8,256]{1,0:T(8,128)S(1)}, f32[8,256]{1,0:T(8,128)S(1)}, u32[]{:S(2)}, u32[]{:S(2)}) collective-permute-start(f32[8,256]{1,0:T(8,128)S(1)} %get-tuple-element.23), channel_id=1, source_target_pairs={{0,8},{8,0},{1,9},{9,1},{2,10},{10,2},{3,11},{11,3},{4,12},{12,4},... | collective-permute-start | bytes 24584 | tf_op jit(solution)/shard_map/ppermute | solution.py:72
  82.5 1.2 %back_c.1.refs_4_.refs_3_ = f32[256,256]{1,0:T(8,128)S(1)} custom-call(f32[256,1024]{1,0:T(8,128)S(1)} %copy-done.2, f32[256,1024]{1,0:T(8,128)S(1)} %collective-permute-done.8.refs_1_.refs_4_, f32[256,1024]{1,0:T(8,128)S(1)} %get-tuple-element.20.refs_2_.refs_1_), custom_call_target="tpu_custom_call" | custom-call | flops 134217728 | bytes 2359296 | tf_op jit(solution)/shard_map/back_c/pallas_call | solution.py:94
  83.7 5.5 %collective-permute-start.12 = (f32[8,256]{1,0:T(8,128)S(1)}, f32[8,256]{1,0:T(8,128)S(1)}, u32[]{:S(2)}, u32[]{:S(2)}) collective-permute-start(f32[8,256]{1,0:T(8,128)S(1)} %get-tuple-element.23), channel_id=1, source_target_pairs={{8,16},{16,8},{9,17},{17,9},{10,18},{18,10},{11,19},{19,11},{12,20... | collective-permute-start | bytes 24584 | tf_op jit(solution)/shard_map/ppermute | solution.py:72
  89.3 1.7 %back_d.1.refs_6_.refs_2_ = f32[256,256]{1,0:T(8,128)S(1)} custom-call(s32[6]{0:T(128)S(1)} %stack.27.refs_0_, f32[256,1024]{1,0:T(8,128)S(1)} %copy-done.2, f32[256,1024]{1,0:T(8,128)S(1)} %collective-permute-done.10.refs_2_.refs_3_, f32[256,1024]{1,0:T(8,128)S(1)} %collective-permute-done.11.refs_3_.refs_4_, f32[256,256]{1,0:T(8,128)S(1)} %back_c.1.refs_4_.refs_3_), custom_call_target="tpu_custom_call" | custom-call | flops 134217728 | bytes 3407896 | tf_op jit(solution)/shard_map/back_d/pallas_call | solution.py:94
  91.0 1.7 %keys_c.1.refs_1_ = f32[256,1024]{1,0:T(8,128)S(1)} custom-call(s32[6]{0:T(128)S(1)} %stack.27.refs_0_, f32[256,1024]{1,0:T(8,128)S(1)} %get-tuple-element.20.refs_2_.refs_1_, f32[256,1024]{1,0:T(8,128)S(1)} %collective-permute-done.7.refs_2_, f32[256,256]{1,0:T(8,128)S(1)} %back_c.1.refs_4_.refs_3_, f32[256,1024]{1,0:T(8,128)S(1)} %collective-permute-done.8.refs_1_.refs_4_, ...), custom_call_target="tpu_custom_call" | custom-call | flops 134217728 | bytes 4464664 | tf_op jit(solution)/shard_map/keys_c/pallas_call | solution.py:94
  92.8 7.2 %collective-permute-done.12.refs_5_ = f32[8,256]{1,0:T(8,128)S(1)} collective-permute-done((f32[8,256]{1,0:T(8,128)S(1)}, f32[8,256]{1,0:T(8,128)S(1)}, u32[]{:S(2)}, u32[]{:S(2)}) %collective-permute-start.12) | collective-permute-done | bytes 8224 | tf_op jit(solution)/shard_map/ppermute | solution.py:72
  100.0 1.7 %keys_d.1.refs_0_ = f32[256,1024]{1,0:T(8,128)S(1)} custom-call(s32[6]{0:T(128)S(1)} %stack.27.refs_0_, f32[256,1024]{1,0:T(8,128)S(1)} %keys_c.1.refs_1_, f32[256,256]{1,0:T(8,128)S(1)} %back_d.1.refs_6_.refs_2_, f32[256,1024]{1,0:T(8,128)S(1)} %collective-permute-done.10.refs_2_.refs_3_, f32[256,1024]{1,0:T(8,128)S(1)} %collective-permute-done.11.refs_3_.refs_4_, ...), custom_call_target="tpu_custom_call" | custom-call | flops 134217728 | bytes 4464664 | tf_op jit(solution)/shard_map/keys_d/pallas_call | solution.py:94
  101.7 1.1 %key_sum.1 = f32[256,1024]{1,0:T(8,128)} custom-call(f32[256,1024]{1,0:T(8,128)S(1)} %keys_d.1.refs_0_, f32[256,1024]{1,0:T(8,128)S(1)} %collective-permute-done.13.refs_1_), custom_call_target="tpu_custom_call" | custom-call | bytes 3145728 | tf_op jit(solution)/shard_map/key_sum/pallas_call | solution.py:94
  (24 shorter events, 0.1 us)
Async XLA Ops:
  0.6 23.4 %collective-permute-start = (f32[256,1024]{1,0:T(8,128)}, f32[256,1024]{1,0:T(8,128)S(1)}, u32[]{:S(2)}, u32[]{:S(2)}) collective-permute-start(f32[256,1024]{1,0:T(8,128)} %refs_1_.3), channel_id=1, source_target_pairs={{0,1},{1,0},{2,3},{3,2},{4,5},{5,4},{6,7},{7,6},{8,9},{9,8},{10,11... | collective-permute-start | bytes 3145736 | tf_op jit(solution)/shard_map/ppermute | solution.py:72
  3.2 22.5 %collective-permute-start.1 = (f32[256,1024]{1,0:T(8,128)}, f32[256,1024]{1,0:T(8,128)}, u32[]{:S(2)}, u32[]{:S(2)}) collective-permute-start(f32[256,1024]{1,0:T(8,128)} %refs_1_.3), channel_id=1, source_target_pairs={{248,56},{249,193},{250,58},{251,195},{252,68},{253,197},{254,70},... | collective-permute-start | bytes 3145736 | tf_op jit(solution)/shard_map/ppermute | solution.py:72
  12.7 34.9 %collective-permute-start.2 = (f32[256,1024]{1,0:T(8,128)}, f32[256,1024]{1,0:T(8,128)S(1)}, u32[]{:S(2)}, u32[]{:S(2)}) collective-permute-start(f32[256,1024]{1,0:T(8,128)} %refs_1_.3), channel_id=1, source_target_pairs={{1,2},{2,1},{3,4},{4,3},{5,6},{6,5},{7,0},{0,7},{9,10},{10,9},{11,... | collective-permute-start | bytes 3145736 | tf_op jit(solution)/shard_map/ppermute | solution.py:72
  19.8 30.8 %collective-permute-start.3 = (f32[256,1024]{1,0:T(8,128)}, f32[256,1024]{1,0:T(8,128)S(1)}, u32[]{:S(2)}, u32[]{:S(2)}) collective-permute-start(f32[256,1024]{1,0:T(8,128)} %refs_1_.3), channel_id=1, source_target_pairs={{0,8},{8,0},{1,9},{9,1},{2,10},{10,2},{3,11},{11,3},{4,12},{12,4},... | collective-permute-start | bytes 3145736 | tf_op jit(solution)/shard_map/ppermute | solution.py:72
  21.7 29.6 %collective-permute-start.6 = (f32[256,1024]{1,0:T(8,128)}, f32[256,1024]{1,0:T(8,128)}, u32[]{:S(2)}, u32[]{:S(2)}) collective-permute-start(f32[256,1024]{1,0:T(8,128)} %refs_2_.1), channel_id=1, source_target_pairs={{248,64},{249,129},{250,66},{251,131},{252,60},{253,197},{254,62},... | collective-permute-start | bytes 3145736 | tf_op jit(solution)/shard_map/ppermute | solution.py:72
  24.0 1.0 copy-start.3
  25.0 28.9 %collective-permute-start.4 = (f32[256,1024]{1,0:T(8,128)}, f32[256,1024]{1,0:T(8,128)S(1)}, u32[]{:S(2)}, u32[]{:S(2)}) collective-permute-start(f32[256,1024]{1,0:T(8,128)} %refs_1_.3), channel_id=1, source_target_pairs={{8,16},{16,8},{9,17},{17,9},{10,18},{18,10},{11,19},{19,11},{12,20... | collective-permute-start | bytes 3145736 | tf_op jit(solution)/shard_map/ppermute | solution.py:72
  25.8 32.5 %collective-permute-start.5 = (f32[256,1024]{1,0:T(8,128)}, f32[256,1024]{1,0:T(8,128)}, u32[]{:S(2)}, u32[]{:S(2)}) collective-permute-start(f32[256,1024]{1,0:T(8,128)} %collective-permute-done.1.refs_3_), channel_id=1, source_target_pairs={{56,256},{193,257},{58,258},{195,259},{68,260},{197,261},{70,262},... | collective-permute-start | bytes 3145736 | tf_op jit(solution)/shard_map/ppermute | solution.py:72
  41.9 1.2 %copy-start = (f32[256,1024]{1,0:T(8,128)S(1)}, f32[256,1024]{1,0:T(8,128)}, u32[]{:S(2)}) copy-start(f32[256,1024]{1,0:T(8,128)} %refs_2_.1) | copy-start | bytes 3145732
  43.1 1.2 %copy-start.1 = (f32[256,1024]{1,0:T(8,128)S(1)}, f32[256,1024]{1,0:T(8,128)}, u32[]{:S(2)}) copy-start(f32[256,1024]{1,0:T(8,128)} %refs_1_.3) | copy-start | bytes 3145732
  44.4 1.2 %copy-start.4 = (f32[256,1024]{1,0:T(8,128)S(1)}, f32[256,1024]{1,0:T(8,128)}, u32[]{:S(2)}) copy-start(f32[256,1024]{1,0:T(8,128)} %copy-done.3) | copy-start | bytes 3145732
  48.7 31.9 %collective-permute-start.8 = (f32[256,1024]{1,0:T(8,128)S(1)}, f32[256,1024]{1,0:T(8,128)S(1)}, u32[]{:S(2)}, u32[]{:S(2)}) collective-permute-start(f32[256,1024]{1,0:T(8,128)S(1)} %get-tuple-element.22), channel_id=1, source_target_pairs={{0,8},{8,0},{1,9},{9,1},{2,10},{10,2},{3,11},{11,3},{4,12},{12,4},... | collective-permute-start | bytes 3145736 | tf_op jit(solution)/shard_map/ppermute | solution.py:72
  50.6 33.1 %collective-permute-start.10 = (f32[256,1024]{1,0:T(8,128)S(1)}, f32[256,1024]{1,0:T(8,128)S(1)}, u32[]{:S(2)}, u32[]{:S(2)}) collective-permute-start(f32[256,1024]{1,0:T(8,128)S(1)} %get-tuple-element.22), channel_id=1, source_target_pairs={{8,16},{16,8},{9,17},{17,9},{10,18},{18,10},{11,19},{19,11},{12,20... | collective-permute-start | bytes 3145736 | tf_op jit(solution)/shard_map/ppermute | solution.py:72
  51.4 37.9 %collective-permute-start.11 = (f32[256,1024]{1,0:T(8,128)}, f32[256,1024]{1,0:T(8,128)S(1)}, u32[]{:S(2)}, u32[]{:S(2)}) collective-permute-start(f32[256,1024]{1,0:T(8,128)} %collective-permute-done.6.refs_10_), channel_id=1, source_target_pairs={{64,256},{129,257},{66,258},{131,259},{60,260},{197,261},{62,262},... | collective-permute-start | bytes 3145736 | tf_op jit(solution)/shard_map/ppermute | solution.py:72
  53.8 4.4 %copy-start.6 = (s32[256]{0:T(256)S(1)}, s32[256]{0:T(256)}, u32[]{:S(2)}) copy-start(s32[256]{0:T(256)} %param.7) | copy-start | bytes 3076
  53.9 4.4 %copy-start.7 = (s32[1,5]{1,0:T(1,128)S(1)}, s32[1,5]{1,0:T(1,128)}, u32[]{:S(2)}) copy-start(s32[1,5]{1,0:T(1,128)} %param.6) | copy-start | bytes 64
  58.3 14.6 %copy-start.2 = (f32[256,1024]{1,0:T(8,128)S(1)}, f32[256,1024]{1,0:T(8,128)}, u32[]{:S(2)}) copy-start(f32[256,1024]{1,0:T(8,128)} %refs_1_.3) | copy-start | bytes 3145732
  58.3 14.6 %copy-start.5 = (f32[256,1024]{1,0:T(8,128)S(1)}, f32[256,1024]{1,0:T(8,128)}, u32[]{:S(2)}) copy-start(f32[256,1024]{1,0:T(8,128)} %copy-done.3) | copy-start | bytes 3145732
  63.9 27.1 %collective-permute-start.7 = (f32[256,1024]{1,0:T(8,128)S(1)}, f32[256,1024]{1,0:T(8,128)S(1)}, u32[]{:S(2)}, u32[]{:S(2)}) collective-permute-start(f32[256,1024]{1,0:T(8,128)S(1)} %get-tuple-element.21), channel_id=1, source_target_pairs={{0,1},{1,0},{2,3},{3,2},{4,5},{5,4},{6,7},{7,6},{8,9},{9,8},{10,11... | collective-permute-start | bytes 3145736 | tf_op jit(solution)/shard_map/ppermute | solution.py:72
  65.8 35.9 %collective-permute-start.13 = (f32[256,1024]{1,0:T(8,128)S(1)}, f32[256,1024]{1,0:T(8,128)S(1)}, u32[]{:S(2)}, u32[]{:S(2)}) collective-permute-start(f32[256,1024]{1,0:T(8,128)S(1)} %get-tuple-element.24), channel_id=1, source_target_pairs={{1,2},{2,1},{3,4},{4,3},{5,6},{6,5},{7,0},{0,7},{9,10},{10,9},{11,... | collective-permute-start | bytes 3145736 | tf_op jit(solution)/shard_map/ppermute | solution.py:72
  80.6 10.4 %collective-permute-start.9 = (f32[8,256]{1,0:T(8,128)S(1)}, f32[8,256]{1,0:T(8,128)S(1)}, u32[]{:S(2)}, u32[]{:S(2)}) collective-permute-start(f32[8,256]{1,0:T(8,128)S(1)} %get-tuple-element.23), channel_id=1, source_target_pairs={{0,8},{8,0},{1,9},{9,1},{2,10},{10,2},{3,11},{11,3},{4,12},{12,4},... | collective-permute-start | bytes 24584 | tf_op jit(solution)/shard_map/ppermute | solution.py:72
  83.7 16.3 %collective-permute-start.12 = (f32[8,256]{1,0:T(8,128)S(1)}, f32[8,256]{1,0:T(8,128)S(1)}, u32[]{:S(2)}, u32[]{:S(2)}) collective-permute-start(f32[8,256]{1,0:T(8,128)S(1)} %get-tuple-element.23), channel_id=1, source_target_pairs={{8,16},{16,8},{9,17},{17,9},{10,18},{18,10},{11,19},{19,11},{12,20... | collective-permute-start | bytes 24584 | tf_op jit(solution)/shard_map/ppermute | solution.py:72

commit v3 on v2

--- a/solution.py
+++ b/solution.py
@@ -277,20 +277,20 @@
         [place, pattern[0], s0, sa, sb, sc, sd, seam, queries, positive[None]],
         smem=2, later=[hop_q], flops=3 * one, name="softmax",
     )
+    (tc,) = score([keys, qc], later=[weights], name="back_c")
+    tb = send(term_b, swap_b)
+    ta = send(term_a, swap_a)
+    aux_c = send(aux, swap_c)
+    aux_d = send(aux, swap_d + seam_swap())
     grad_queries, own = call(
         query_gradient,
         [(t, d), (t, d)],
         [place, weights, queries, keys, ka, kb, kc, kd, seam],
-        smem=1, flops=6 * one, name="query_gradient",
-    )
-    (tc,) = score([keys, qc], later=[own], name="back_c")
-    tb = send(term_b, swap_b)
-    ta = send(term_a, swap_a)
-    aux_c = send(aux, swap_c)
-    aux_d = send(aux, swap_d + seam_swap())
+        smem=1, later=[tc], flops=6 * one, name="query_gradient",
+    )
     (td,) = call(
         functools.partial(seam_or, sharpness), [(t, t)],
-        [place, keys, qd, seam_q], smem=1, later=[tc], flops=one, name="back_d",
+        [place, keys, qd, seam_q], smem=1, later=[own], flops=one, name="back_d",
     )
     (some,) = call(
         functools.partial(keys_c, sharpness), [(t, d)],

time: 104 us -> 104 us (level)
  the two profiles are of different devices: /device:TPU:49 before, /device:TPU:59 now
where the time goes in v3:
time: 104 us; the launch traced here: 102 us
  starting transfers between devices  61 us (59%)
  Pallas kernels  29 us (28%)
  waiting for transfers between devices  7.05 us (7%)
  local copies, waits for them, and re-layouts  4.27 us (4%)
    ppermute x14, starting transfers between devices, send(): return lax.ppermute(value, AXES, pairs)  61 us
    pallas_call x11, Pallas kernels, call(): pl.pallas_call(run, out_shape=out, in_specs=[scalar] * smem + [vmem] * co...  29 us
    ppermute x14, waiting for transfers between devices, send(): return lax.ppermute(value, AXES, pairs)  7.05 us
    unnamed x24, local copies, waits for them, and re-layouts  4.18 us
  transfers between devices with their start and end apart: 14, of which 2 were waited for; matrix products, arithmetic and copies ran while one was open for 0% of the time, Pallas kernels for 27%

profile of v3, /device:TPU:59, one launch (start us, length us, event | category | flops | bytes accessed | tf_op | source)
XLA Modules:
  0.0 102.3 jit_solution(16714764102437666606)
XLA Ops:
  0.6 2.6 %collective-permute-start = (f32[256,1024]{1,0:T(8,128)}, f32[256,1024]{1,0:T(8,128)S(1)}, u32[]{:S(2)}, u32[]{:S(2)}) collective-permute-start(f32[256,1024]{1,0:T(8,128)} %refs_1_.3), channel_id=1, source_target_pairs={{0,1},{1,0},{2,3},{3,2},{4,5},{5,4},{6,7},{7,6},{8,9},{9,8},{10,11... | collective-permute-start | bytes 3145736 | tf_op jit(solution)/shard_map/ppermute | solution.py:72
  3.2 1.7 %collective-permute-start.1 = (f32[256,1024]{1,0:T(8,128)}, f32[256,1024]{1,0:T(8,128)}, u32[]{:S(2)}, u32[]{:S(2)}) collective-permute-start(f32[256,1024]{1,0:T(8,128)} %refs_1_.3), channel_id=1, source_target_pairs={{248,56},{249,193},{250,58},{251,195},{252,68},{253,197},{254,70},... | collective-permute-start | bytes 3145736 | tf_op jit(solution)/shard_map/ppermute | solution.py:72
  4.9 4.4 %collective-permute-start.2 = (f32[256,1024]{1,0:T(8,128)}, f32[256,1024]{1,0:T(8,128)S(1)}, u32[]{:S(2)}, u32[]{:S(2)}) collective-permute-start(f32[256,1024]{1,0:T(8,128)} %refs_1_.3), channel_id=1, source_target_pairs={{1,2},{2,1},{3,4},{4,3},{5,6},{6,5},{7,0},{0,7},{9,10},{10,9},{11,... | collective-permute-start | bytes 3145736 | tf_op jit(solution)/shard_map/ppermute | solution.py:72
  9.3 4.0 %collective-permute-start.3 = (f32[256,1024]{1,0:T(8,128)}, f32[256,1024]{1,0:T(8,128)}, u32[]{:S(2)}, u32[]{:S(2)}) collective-permute-start(f32[256,1024]{1,0:T(8,128)} %refs_1_.3), channel_id=1, source_target_pairs={{0,8},{8,0},{1,9},{9,1},{2,10},{10,2},{3,11},{11,3},{4,12},{12,4},... | collective-permute-start | bytes 3145736 | tf_op jit(solution)/shard_map/ppermute | solution.py:72
  13.3 1.7 %collective-permute-start.6 = (f32[256,1024]{1,0:T(8,128)}, f32[256,1024]{1,0:T(8,128)}, u32[]{:S(2)}, u32[]{:S(2)}) collective-permute-start(f32[256,1024]{1,0:T(8,128)} %refs_2_.1), channel_id=1, source_target_pairs={{248,64},{249,129},{250,66},{251,131},{252,60},{253,197},{254,62},... | collective-permute-start | bytes 3145736 | tf_op jit(solution)/shard_map/ppermute | solution.py:72
  15.0 8.8 %collective-permute-start.4 = (f32[256,1024]{1,0:T(8,128)}, f32[256,1024]{1,0:T(8,128)}, u32[]{:S(2)}, u32[]{:S(2)}) collective-permute-start(f32[256,1024]{1,0:T(8,128)} %refs_1_.3), channel_id=1, source_target_pairs={{8,16},{16,8},{9,17},{17,9},{10,18},{18,10},{11,19},{19,11},{12,20... | collective-permute-start | bytes 3145736 | tf_op jit(solution)/shard_map/ppermute | solution.py:72
  23.8 1.7 %collective-permute-start.5 = (f32[256,1024]{1,0:T(8,128)}, f32[256,1024]{1,0:T(8,128)}, u32[]{:S(2)}, u32[]{:S(2)}) collective-permute-start(f32[256,1024]{1,0:T(8,128)} %collective-permute-done.1.refs_3_), channel_id=1, source_target_pairs={{56,256},{193,257},{58,258},{195,259},{68,260},{197,261},{70,262},... | collective-permute-start | bytes 3145736 | tf_op jit(solution)/shard_map/ppermute | solution.py:72
  25.5 1.2 %copy-done = f32[256,1024]{1,0:T(8,128)S(1)} copy-done((f32[256,1024]{1,0:T(8,128)S(1)}, f32[256,1024]{1,0:T(8,128)}, u32[]{:S(2)}) %copy-start) | copy-done | bytes 1048600
  26.7 1.2 %copy-done.2 = f32[256,1024]{1,0:T(8,128)S(1)} copy-done((f32[256,1024]{1,0:T(8,128)S(1)}, f32[256,1024]{1,0:T(8,128)}, u32[]{:S(2)}) %copy-start.2) | copy-done | bytes 1048600
  28.0 1.9 %first_scores.1 = (f32[256,256]{1,0:T(8,128)S(1)}, f32[256,256]{1,0:T(8,128)S(1)}) custom-call(f32[256,1024]{1,0:T(8,128)S(1)} %copy-done, f32[256,1024]{1,0:T(8,128)S(1)} %copy-done.2, f32[256,1024]{1,0:T(8,128)S(1)} %collective-permute-done.refs_2_.refs_4_, f32[256,1024]{1,0:T(8,128)} %collective-permute-done.1.refs_3_), custom_call_target="tpu_custom_call" | custom-call | flops 268435456 | bytes 3670016 | tf_op jit(solution)/shard_map/first_scores/pallas_call | solution.py:94
  29.9 3.8 %collective-permute-done.2.refs_1_.refs_5_ = f32[256,1024]{1,0:T(8,128)S(1)} collective-permute-done((f32[256,1024]{1,0:T(8,128)}, f32[256,1024]{1,0:T(8,128)S(1)}, u32[]{:S(2)}, u32[]{:S(2)}) %collective-permute-start.2) | collective-permute-done | bytes 1048608 | tf_op jit(solution)/shard_map/ppermute | solution.py:72
  33.7 2.1 %scores_b.1 = (f32[256,256]{1,0:T(8,128)S(1)}, f32[256,1024]{1,0:T(8,128)}) custom-call(f32[256,1024]{1,0:T(8,128)S(1)} %copy-done, f32[256,1024]{1,0:T(8,128)S(1)} %collective-permute-done.2.refs_1_.refs_5_, f32[256,256]{1,0:T(8,128)S(1)} %get-tuple-element.14.refs_2_), custom_call_target="tpu_custom_call" | custom-call | flops 134217728 | bytes 3407872 | tf_op jit(solution)/shard_map/scores_b/pallas_call | solution.py:94
  35.8 0.7 copy-done.6
  36.6 3.6 %collective-permute-start.7 = (f32[256,1024]{1,0:T(8,128)}, f32[256,1024]{1,0:T(8,128)S(1)}, u32[]{:S(2)}, u32[]{:S(2)}) collective-permute-start(f32[256,1024]{1,0:T(8,128)} %get-tuple-element.19), channel_id=1, source_target_pairs={{0,8},{8,0},{1,9},{9,1},{2,10},{10,2},{3,11},{11,3},{4,12},{12,4},... | collective-permute-start | bytes 3145736 | tf_op jit(solution)/shard_map/ppermute | solution.py:72
  40.2 0.1 stack.27.refs_0_
  40.3 18.2 %collective-permute-start.10 = (f32[256,1024]{1,0:T(8,128)}, f32[256,1024]{1,0:T(8,128)S(1)}, u32[]{:S(2)}, u32[]{:S(2)}) collective-permute-start(f32[256,1024]{1,0:T(8,128)} %get-tuple-element.19), channel_id=1, source_target_pairs={{8,16},{16,8},{9,17},{17,9},{10,18},{18,10},{11,19},{19,11},{12,20... | collective-permute-start | bytes 3145736 | tf_op jit(solution)/shard_map/ppermute | solution.py:72
  58.5 0.7 collective-permute-start.11
  59.2 0.9 copy-done.7
  60.2 2.4 %scores_c.1.refs_2_.refs_5_ = f32[256,256]{1,0:T(8,128)S(1)} custom-call(f32[256,1024]{1,0:T(8,128)S(1)} %copy-done.1, f32[256,1024]{1,0:T(8,128)} %collective-permute-done.3.refs_1_.refs_6_, f32[256,256]{1,0:T(8,128)S(1)} %copy-done.7), custom_call_target="tpu_custom_call" | custom-call | flops 134217728 | bytes 2359296 | tf_op jit(solution)/shard_map/scores_c/pallas_call | solution.py:94
  62.6 2.4 %scores_d.1.refs_6_ = f32[256,256]{1,0:T(8,128)S(1)} custom-call(f32[256,1024]{1,0:T(8,128)S(1)} %copy-done.1, f32[256,1024]{1,0:T(8,128)} %collective-permute-done.4.refs_1_.refs_7_, f32[256,256]{1,0:T(8,128)S(1)} %scores_c.1.refs_2_.refs_5_), custom_call_target="tpu_custom_call" | custom-call | flops 134217728 | bytes 2359296 | tf_op jit(solution)/shard_map/scores_d/pallas_call | solution.py:94
  65.1 4.4 %softmax.1 = (f32[256,1280]{1,0:T(8,128)S(1)}, f32[1,256]{1,0:T(1,128)}, f32[8,256]{1,0:T(8,128)S(1)}, f32[256,1024]{1,0:T(8,128)S(1)}, f32[256,1024]{1,0:T(8,128)S(1)}) custom-call(s32[6]{0:T(128)S(1)} %stack.27.refs_0_, s32[5]{0:T(128)S(1)} %bitcast.9, f32[256,256]{1,0:T(8,128)S(1)} %get-tuple-element.14.refs_2_, f32[256,256]{1,0:T(8,128)S(1)} %copy-done.9, ...), custom_call_target="tpu_custom_call" | custom-call | flops 402653184 | bytes 6826028 | tf_op jit(solution)/shard_map/softmax/pallas_call | solution.py:94
  69.5 1.9 %collective-permute-start.8 = (f32[256,1024]{1,0:T(8,128)S(1)}, f32[256,1024]{1,0:T(8,128)S(1)}, u32[]{:S(2)}, u32[]{:S(2)}) collective-permute-start(f32[256,1024]{1,0:T(8,128)S(1)} %get-tuple-element.22), channel_id=1, source_target_pairs={{0,1},{1,0},{2,3},{3,2},{4,5},{5,4},{6,7},{7,6},{8,9},{9,8},{10,11... | collective-permute-start | bytes 3145736 | tf_op jit(solution)/shard_map/ppermute | solution.py:72
  71.4 6.3 %collective-permute-start.13 = (f32[256,1024]{1,0:T(8,128)S(1)}, f32[256,1024]{1,0:T(8,128)S(1)}, u32[]{:S(2)}, u32[]{:S(2)}) collective-permute-start(f32[256,1024]{1,0:T(8,128)S(1)} %get-tuple-element.24), channel_id=1, source_target_pairs={{1,2},{2,1},{3,4},{4,3},{5,6},{6,5},{7,0},{0,7},{9,10},{10,9},{11,... | collective-permute-start | bytes 3145736 | tf_op jit(solution)/shard_map/ppermute | solution.py:72
  77.7 2.1 %collective-permute-start.9 = (f32[8,256]{1,0:T(8,128)S(1)}, f32[8,256]{1,0:T(8,128)S(1)}, u32[]{:S(2)}, u32[]{:S(2)}) collective-permute-start(f32[8,256]{1,0:T(8,128)S(1)} %get-tuple-element.23), channel_id=1, source_target_pairs={{0,8},{8,0},{1,9},{9,1},{2,10},{10,2},{3,11},{11,3},{4,12},{12,4},... | collective-permute-start | bytes 24584 | tf_op jit(solution)/shard_map/ppermute | solution.py:72
  79.9 1.2 %back_c.1.refs_9_.refs_3_ = f32[256,256]{1,0:T(8,128)S(1)} custom-call(f32[256,1024]{1,0:T(8,128)S(1)} %copy-done.3, f32[256,1024]{1,0:T(8,128)S(1)} %collective-permute-done.7.refs_1_.refs_4_, f32[256,1280]{1,0:T(8,128)S(1)} %get-tuple-element.18.refs_2_.refs_1_), custom_call_target="tpu_custom_call" | custom-call | flops 134217728 | bytes 2359296 | tf_op jit(solution)/shard_map/back_c/pallas_call | solution.py:94
  81.1 8.4 %query_gradient.1 = (f32[256,1024]{1,0:T(8,128)}, f32[256,1024]{1,0:T(8,128)S(1)}) custom-call(s32[6]{0:T(128)S(1)} %stack.27.refs_0_, f32[256,1280]{1,0:T(8,128)S(1)} %get-tuple-element.18.refs_2_.refs_1_, f32[256,1024]{1,0:T(8,128)S(1)} %copy-done.1, f32[256,1024]{1,0:T(8,128)S(1)} %copy-done.3, f32[256,1024]{1,0:T(8,128)S(1)} %copy-done.5, ...), custom_call_target="tpu_custom_call" | custom-call | flops 805306368 | bytes 10747928 | tf_op jit(solution)/shard_map/query_gradient/pallas_call | solution.py:94
  89.5 3.3 %collective-permute-start.12 = (f32[8,256]{1,0:T(8,128)S(1)}, f32[8,256]{1,0:T(8,128)S(1)}, u32[]{:S(2)}, u32[]{:S(2)}) collective-permute-start(f32[8,256]{1,0:T(8,128)S(1)} %get-tuple-element.23), channel_id=1, source_target_pairs={{8,16},{16,8},{9,17},{17,9},{10,18},{18,10},{11,19},{19,11},{12,20... | collective-permute-start | bytes 24584 | tf_op jit(solution)/shard_map/ppermute | solution.py:72
  92.8 1.7 %back_d.1.refs_6_.refs_2_ = f32[256,256]{1,0:T(8,128)S(1)} custom-call(s32[6]{0:T(128)S(1)} %stack.27.refs_0_, f32[256,1024]{1,0:T(8,128)S(1)} %copy-done.3, f32[256,1024]{1,0:T(8,128)S(1)} %collective-permute-done.10.refs_2_.refs_3_, f32[256,1024]{1,0:T(8,128)S(1)} %collective-permute-done.11.refs_3_.refs_4_, f32[256,1024]{1,0:T(8,128)S(1)} %get-tuple-element.21.refs_4_.refs_1_), custom_call_target="tpu_custom_call" | custom-call | flops 134217728 | bytes 3407896 | tf_op jit(solution)/shard_map/back_d/pallas_call | solution.py:94
  94.6 1.7 %keys_c.1.refs_1_ = f32[256,1024]{1,0:T(8,128)S(1)} custom-call(s32[6]{0:T(128)S(1)} %stack.27.refs_0_, f32[256,1024]{1,0:T(8,128)S(1)} %get-tuple-element.21.refs_4_.refs_1_, f32[256,1024]{1,0:T(8,128)S(1)} %collective-permute-done.8.refs_2_, f32[256,256]{1,0:T(8,128)S(1)} %back_c.1.refs_9_.refs_3_, f32[256,1024]{1,0:T(8,128)S(1)} %collective-permute-done.7.refs_1_.refs_4_, ...), custom_call_target="tpu_custom_call" | custom-call | flops 134217728 | bytes 4464664 | tf_op jit(solution)/shard_map/keys_c/pallas_call | solution.py:94
  96.3 1.7 %keys_d.1.refs_0_ = f32[256,1024]{1,0:T(8,128)S(1)} custom-call(s32[6]{0:T(128)S(1)} %stack.27.refs_0_, f32[256,1024]{1,0:T(8,128)S(1)} %keys_c.1.refs_1_, f32[256,256]{1,0:T(8,128)S(1)} %back_d.1.refs_6_.refs_2_, f32[256,1024]{1,0:T(8,128)S(1)} %collective-permute-done.10.refs_2_.refs_3_, f32[256,1024]{1,0:T(8,128)S(1)} %collective-permute-done.11.refs_3_.refs_4_, ...), custom_call_target="tpu_custom_call" | custom-call | flops 134217728 | bytes 4464664 | tf_op jit(solution)/shard_map/keys_d/pallas_call | solution.py:94
  98.0 3.2 %collective-permute-done.13.refs_1_ = f32[256,1024]{1,0:T(8,128)S(1)} collective-permute-done((f32[256,1024]{1,0:T(8,128)S(1)}, f32[256,1024]{1,0:T(8,128)S(1)}, u32[]{:S(2)}, u32[]{:S(2)}) %collective-permute-start.13) | collective-permute-done | bytes 1048608 | tf_op jit(solution)/shard_map/ppermute | solution.py:72
  101.2 1.1 %key_sum.1 = f32[256,1024]{1,0:T(8,128)} custom-call(f32[256,1024]{1,0:T(8,128)S(1)} %keys_d.1.refs_0_, f32[256,1024]{1,0:T(8,128)S(1)} %collective-permute-done.13.refs_1_), custom_call_target="tpu_custom_call" | custom-call | bytes 3145728 | tf_op jit(solution)/shard_map/key_sum/pallas_call | solution.py:94
  (32 shorter events, 0.1 us)
Async XLA Ops:
  0.6 14.4 %collective-permute-start = (f32[256,1024]{1,0:T(8,128)}, f32[256,1024]{1,0:T(8,128)S(1)}, u32[]{:S(2)}, u32[]{:S(2)}) collective-permute-start(f32[256,1024]{1,0:T(8,128)} %refs_1_.3), channel_id=1, source_target_pairs={{0,1},{1,0},{2,3},{3,2},{4,5},{5,4},{6,7},{7,6},{8,9},{9,8},{10,11... | collective-permute-start | bytes 3145736 | tf_op jit(solution)/shard_map/ppermute | solution.py:72
  3.2 20.6 %collective-permute-start.1 = (f32[256,1024]{1,0:T(8,128)}, f32[256,1024]{1,0:T(8,128)}, u32[]{:S(2)}, u32[]{:S(2)}) collective-permute-start(f32[256,1024]{1,0:T(8,128)} %refs_1_.3), channel_id=1, source_target_pairs={{248,56},{249,193},{250,58},{251,195},{252,68},{253,197},{254,70},... | collective-permute-start | bytes 3145736 | tf_op jit(solution)/shard_map/ppermute | solution.py:72
  4.9 28.8 %collective-permute-start.2 = (f32[256,1024]{1,0:T(8,128)}, f32[256,1024]{1,0:T(8,128)S(1)}, u32[]{:S(2)}, u32[]{:S(2)}) collective-permute-start(f32[256,1024]{1,0:T(8,128)} %refs_1_.3), channel_id=1, source_target_pairs={{1,2},{2,1},{3,4},{4,3},{5,6},{6,5},{7,0},{0,7},{9,10},{10,9},{11,... | collective-permute-start | bytes 3145736 | tf_op jit(solution)/shard_map/ppermute | solution.py:72
  9.3 31.0 %collective-permute-start.3 = (f32[256,1024]{1,0:T(8,128)}, f32[256,1024]{1,0:T(8,128)}, u32[]{:S(2)}, u32[]{:S(2)}) collective-permute-start(f32[256,1024]{1,0:T(8,128)} %refs_1_.3), channel_id=1, source_target_pairs={{0,8},{8,0},{1,9},{9,1},{2,10},{10,2},{3,11},{11,3},{4,12},{12,4},... | collective-permute-start | bytes 3145736 | tf_op jit(solution)/shard_map/ppermute | solution.py:72
  13.3 45.1 %collective-permute-start.6 = (f32[256,1024]{1,0:T(8,128)}, f32[256,1024]{1,0:T(8,128)}, u32[]{:S(2)}, u32[]{:S(2)}) collective-permute-start(f32[256,1024]{1,0:T(8,128)} %refs_2_.1), channel_id=1, source_target_pairs={{248,64},{249,129},{250,66},{251,131},{252,60},{253,197},{254,62},... | collective-permute-start | bytes 3145736 | tf_op jit(solution)/shard_map/ppermute | solution.py:72
  15.0 14.9 %copy-start.4 = (f32[256,1024]{1,0:T(8,128)}, f32[256,1024]{1,0:T(8,128)S(1)}, u32[]{:S(2)}) copy-start(f32[256,1024]{1,0:T(8,128)S(1)} %collective-permute-done.refs_2_.refs_4_) | copy-start | bytes 3145732
  15.0 47.6 %collective-permute-start.4 = (f32[256,1024]{1,0:T(8,128)}, f32[256,1024]{1,0:T(8,128)}, u32[]{:S(2)}, u32[]{:S(2)}) collective-permute-start(f32[256,1024]{1,0:T(8,128)} %refs_1_.3), channel_id=1, source_target_pairs={{8,16},{16,8},{9,17},{17,9},{10,18},{18,10},{11,19},{19,11},{12,20... | collective-permute-start | bytes 3145736 | tf_op jit(solution)/shard_map/ppermute | solution.py:72
  23.8 41.2 %collective-permute-start.5 = (f32[256,1024]{1,0:T(8,128)}, f32[256,1024]{1,0:T(8,128)}, u32[]{:S(2)}, u32[]{:S(2)}) collective-permute-start(f32[256,1024]{1,0:T(8,128)} %collective-permute-done.1.refs_3_), channel_id=1, source_target_pairs={{56,256},{193,257},{58,258},{195,259},{68,260},{197,261},{70,262},... | collective-permute-start | bytes 3145736 | tf_op jit(solution)/shard_map/ppermute | solution.py:72
  25.5 1.2 %copy-start = (f32[256,1024]{1,0:T(8,128)S(1)}, f32[256,1024]{1,0:T(8,128)}, u32[]{:S(2)}) copy-start(f32[256,1024]{1,0:T(8,128)} %refs_2_.1) | copy-start | bytes 3145732
  26.7 1.2 %copy-start.2 = (f32[256,1024]{1,0:T(8,128)S(1)}, f32[256,1024]{1,0:T(8,128)}, u32[]{:S(2)}) copy-start(f32[256,1024]{1,0:T(8,128)} %refs_1_.3) | copy-start | bytes 3145732
  29.9 5.9 %copy-start.8 = (f32[256,256]{1,0:T(8,128)}, f32[256,256]{1,0:T(8,128)S(1)}, u32[]{:S(2)}) copy-start(f32[256,256]{1,0:T(8,128)S(1)} %get-tuple-element.15.refs_3_) | copy-start | bytes 786436
  29.9 29.3 %copy-start.1 = (f32[256,1024]{1,0:T(8,128)S(1)}, f32[256,1024]{1,0:T(8,128)}, u32[]{:S(2)}) copy-start(f32[256,1024]{1,0:T(8,128)} %refs_2_.1) | copy-start | bytes 3145732
  35.8 0.7 copy-start.6
  36.6 41.2 %collective-permute-start.7 = (f32[256,1024]{1,0:T(8,128)}, f32[256,1024]{1,0:T(8,128)S(1)}, u32[]{:S(2)}, u32[]{:S(2)}) collective-permute-start(f32[256,1024]{1,0:T(8,128)} %get-tuple-element.19), channel_id=1, source_target_pairs={{0,8},{8,0},{1,9},{9,1},{2,10},{10,2},{3,11},{11,3},{4,12},{12,4},... | collective-permute-start | bytes 3145736 | tf_op jit(solution)/shard_map/ppermute | solution.py:72
  40.3 49.2 %collective-permute-start.10 = (f32[256,1024]{1,0:T(8,128)}, f32[256,1024]{1,0:T(8,128)S(1)}, u32[]{:S(2)}, u32[]{:S(2)}) collective-permute-start(f32[256,1024]{1,0:T(8,128)} %get-tuple-element.19), channel_id=1, source_target_pairs={{8,16},{16,8},{9,17},{17,9},{10,18},{18,10},{11,19},{19,11},{12,20... | collective-permute-start | bytes 3145736 | tf_op jit(solution)/shard_map/ppermute | solution.py:72
  58.5 34.4 %collective-permute-start.11 = (f32[256,1024]{1,0:T(8,128)}, f32[256,1024]{1,0:T(8,128)S(1)}, u32[]{:S(2)}, u32[]{:S(2)}) collective-permute-start(f32[256,1024]{1,0:T(8,128)} %collective-permute-done.6.refs_10_), channel_id=1, source_target_pairs={{64,256},{129,257},{66,258},{131,259},{60,260},{197,261},{62,262},... | collective-permute-start | bytes 3145736 | tf_op jit(solution)/shard_map/ppermute | solution.py:72
  59.2 1.0 copy-start.7
  62.6 2.5 %copy-start.9 = (f32[256,256]{1,0:T(8,128)S(1)}, f32[256,256]{1,0:T(8,128)}, u32[]{:S(2)}) copy-start(f32[256,256]{1,0:T(8,128)} %copy-done.8) | copy-start | bytes 786436
  62.6 2.5 %copy-start.10 = (s32[256]{0:T(256)S(1)}, s32[256]{0:T(256)}, u32[]{:S(2)}) copy-start(s32[256]{0:T(256)} %param.7) | copy-start | bytes 3076
  62.6 2.5 %copy-start.11 = (s32[1,5]{1,0:T(1,128)S(1)}, s32[1,5]{1,0:T(1,128)}, u32[]{:S(2)}) copy-start(s32[1,5]{1,0:T(1,128)} %param.6) | copy-start | bytes 64
  65.1 14.8 %copy-start.3 = (f32[256,1024]{1,0:T(8,128)S(1)}, f32[256,1024]{1,0:T(8,128)}, u32[]{:S(2)}) copy-start(f32[256,1024]{1,0:T(8,128)} %refs_1_.3) | copy-start | bytes 3145732
  69.5 25.1 %collective-permute-start.8 = (f32[256,1024]{1,0:T(8,128)S(1)}, f32[256,1024]{1,0:T(8,128)S(1)}, u32[]{:S(2)}, u32[]{:S(2)}) collective-permute-start(f32[256,1024]{1,0:T(8,128)S(1)} %get-tuple-element.22), channel_id=1, source_target_pairs={{0,1},{1,0},{2,3},{3,2},{4,5},{5,4},{6,7},{7,6},{8,9},{9,8},{10,11... | collective-permute-start | bytes 3145736 | tf_op jit(solution)/shard_map/ppermute | solution.py:72
  71.4 29.9 %collective-permute-start.13 = (f32[256,1024]{1,0:T(8,128)S(1)}, f32[256,1024]{1,0:T(8,128)S(1)}, u32[]{:S(2)}, u32[]{:S(2)}) collective-permute-start(f32[256,1024]{1,0:T(8,128)S(1)} %get-tuple-element.24), channel_id=1, source_target_pairs={{1,2},{2,1},{3,4},{4,3},{5,6},{6,5},{7,0},{0,7},{9,10},{10,9},{11,... | collective-permute-start | bytes 3145736 | tf_op jit(solution)/shard_map/ppermute | solution.py:72
  77.7 16.9 %collective-permute-start.9 = (f32[8,256]{1,0:T(8,128)S(1)}, f32[8,256]{1,0:T(8,128)S(1)}, u32[]{:S(2)}, u32[]{:S(2)}) collective-permute-start(f32[8,256]{1,0:T(8,128)S(1)} %get-tuple-element.23), channel_id=1, source_target_pairs={{0,8},{8,0},{1,9},{9,1},{2,10},{10,2},{3,11},{11,3},{4,12},{12,4},... | collective-permute-start | bytes 24584 | tf_op jit(solution)/shard_map/ppermute | solution.py:72
  79.9 1.2 %copy-start.5 = (f32[256,1024]{1,0:T(8,128)S(1)}, f32[256,1024]{1,0:T(8,128)}, u32[]{:S(2)}) copy-start(f32[256,1024]{1,0:T(8,128)} %copy-done.4) | copy-start | bytes 3145732
  89.5 6.8 %collective-permute-start.12 = (f32[8,256]{1,0:T(8,128)S(1)}, f32[8,256]{1,0:T(8,128)S(1)}, u32[]{:S(2)}, u32[]{:S(2)}) collective-permute-start(f32[8,256]{1,0:T(8,128)S(1)} %get-tuple-element.23), channel_id=1, source_target_pairs={{8,16},{16,8},{9,17},{17,9},{10,18},{18,10},{11,19},{19,11},{12,20... | collective-permute-start | bytes 24584 | tf_op jit(solution)/shard_map/ppermute | solution.py:72
